TPU v7x, 256 devices: a whole 4x4x8 slice. The times are simulated.
256 devices in a mesh: dp: 8 (over y_lo, x), fsdp: 32 (over y_hi, z, core).
Axes of the slice: x: 4, y: 4 (y_hi: 2, y_lo: 2; y = y_hi * 2 + y_lo), z: 8, core: 2. Of those that a mesh axis runs over, the one named last changes fastest.
Arguments:
- patches: bfloat16 [32768, 1280], P(('dp', 'fsdp')), may hold values from -6 to 6
- cotangent: bfloat16 [32768, 1280], P(('dp', 'fsdp')), may hold values from -24 to 24
- tile_counts: int32 [256], P(('dp', 'fsdp')), may hold values from 0 to 4, as said below
- ln_gain: float32 [1280], replicated, may hold values from 0.25 to 4
- qkv_weight: bfloat16 [1280, 1920], P('fsdp'), may hold values from -2 to 2
- out_weight: bfloat16 [640, 1280], P('fsdp'), may hold values from -0.25 to 0.25
- text_states: bfloat16 [1024, 8192], P('dp'), may hold values from -6 to 6
- mask_ids: int32 [1024], P('dp'), may hold values from 0 to 32
- text_lengths: int32 [8], P('dp'), may hold values from 1 to 128
- gate_value: float32 [1], replicated, may hold values from -1.5 to 1.5
- query_weight: bfloat16 [8192, 8192], P(None, 'fsdp'), may hold values from -1 to 1
- kv_weight: bfloat16 [1280, 2048], P('fsdp'), may hold values from -2 to 2
- output_weight: bfloat16 [8192, 8192], P('fsdp'), may hold values from -0.25 to 0.25
Outputs:
- grad_qkv: float32 [1280, 1920], P('fsdp')
- grad_out: float32 [640, 1280], P('fsdp')
- cross_out: bfloat16 [1024, 8192], P('dp', 'fsdp')
Inputs may be any that keep to these rules, and one draw needn't show every extreme that they name: `tile_counts`: some image has 4 live tiles and some has none.
All inputs are finite; a program needn't handle non-finite values.
Results may differ from a plain program's by a relative error of at most 0.024.
The roundings to bfloat16 on the way count: a program that leaves them out, or rounds other values in their place, can miss the bound.
Values may be sent and summed in bfloat16 or wider, within the bound.
A program may use at most 128 MiB of HBM per device.

v0:
```python
import jax
import jax.numpy as jnp
from jax import lax
from jax.sharding import PartitionSpec as P

EH = 8
PATCH = 32
HD = 128
KVH = 8


EPS = 1e-05
NEG = -1e30


def encode(patch_piece, ln_gain, qkv_weight, out_weight, tile_count):
    row_count = patch_piece.shape[0]
    head_width = out_weight.shape[0]
    head_size = head_width // EH
    inputs_f = patch_piece.astype(jnp.float32)
    row_mean = jnp.mean(inputs_f, axis=-1, keepdims=True)
    centred = inputs_f - row_mean
    spread = jnp.mean(centred * centred, axis=-1, keepdims=True)
    normed = (centred * lax.rsqrt(spread + EPS) * ln_gain).astype(jnp.bfloat16)
    joined_qkv = jnp.dot(normed, qkv_weight, preferred_element_type=jnp.float32).astype(
        jnp.bfloat16
    )
    joined_qkv = joined_qkv.reshape(row_count, 3, EH, head_size)
    queries = joined_qkv[:, 0]
    key_rows = joined_qkv[:, 1]
    value_rows = joined_qkv[:, 2]
    live_rows = jnp.arange(row_count) // PATCH < tile_count
    scores = jnp.einsum(
        "qhd,khd->hqk", queries, key_rows, preferred_element_type=jnp.float32
    ) * head_size ** (-0.5)
    scores = jnp.where(live_rows[None, None, :], scores, NEG)
    row_top = jnp.max(scores, axis=-1, keepdims=True)
    weights = jnp.exp(scores - row_top)
    attn_probs = weights / jnp.sum(weights, axis=-1, keepdims=True)
    attn_low = attn_probs.astype(jnp.bfloat16)
    context = jnp.einsum("hqk,khd->qhd", attn_low, value_rows, preferred_element_type=jnp.float32)
    context = context.astype(jnp.bfloat16).reshape(row_count, head_width)
    branch = jnp.dot(context, out_weight, preferred_element_type=jnp.float32)
    vision = jnp.where(live_rows[:, None], inputs_f + branch, 0.0).astype(jnp.bfloat16)
    return (
        vision,
        (normed, queries, key_rows, value_rows, attn_probs, attn_low, context, live_rows),
    )


def encode_grads(saved, out_weight, cotangent):
    normed, queries, key_rows, value_rows, attn_probs, attn_low, context, live_rows = saved
    row_count, head_count, head_size = queries.shape
    upstream = jnp.where(live_rows[:, None], cotangent, jnp.zeros_like(cotangent))
    grad_out = lax.dot_general(
        context, upstream, (((0,), (0,)), ((), ())), preferred_element_type=jnp.float32
    )
    grad_context = lax.dot_general(
        upstream, out_weight, (((1,), (1,)), ((), ())), preferred_element_type=jnp.float32
    )
    grad_context = grad_context.astype(jnp.bfloat16).reshape(row_count, head_count, head_size)
    grad_probs = jnp.einsum(
        "qhd,khd->hqk", grad_context, value_rows, preferred_element_type=jnp.float32
    )
    grad_values = jnp.einsum(
        "hqk,qhd->khd", attn_low, grad_context, preferred_element_type=jnp.float32
    )
    inner_sum = jnp.sum(attn_probs * grad_probs, axis=-1, keepdims=True)
    grad_scores = (attn_probs * (grad_probs - inner_sum) * head_size ** (-0.5)).astype(jnp.bfloat16)
    grad_queries = jnp.einsum(
        "hqk,khd->qhd", grad_scores, key_rows, preferred_element_type=jnp.float32
    )
    grad_keys = jnp.einsum("hqk,qhd->khd", grad_scores, queries, preferred_element_type=jnp.float32)
    grad_joined = jnp.stack([grad_queries, grad_keys, grad_values], axis=1).astype(jnp.bfloat16)
    grad_joined = grad_joined.reshape(row_count, 3 * head_count * head_size)
    grad_qkv = lax.dot_general(
        normed, grad_joined, (((0,), (0,)), ((), ())), preferred_element_type=jnp.float32
    )
    return (grad_qkv, grad_out)


def per_device(
    patches,
    cotangent,
    tile_counts,
    ln_gain,
    qkv_weight,
    out_weight,
    text_states,
    mask_ids,
    text_lengths,
    gate_value,
    query_weight,
    kv_weight,
    output_weight,
):
    groups = lax.axis_size("fsdp")
    fsdp_index = lax.axis_index("fsdp")
    row_count = patches.shape[0]
    full_qkv, full_out, full_kv = (
        lax.all_gather(qkv_weight, "fsdp", axis=0, tiled=True),
        lax.all_gather(out_weight, "fsdp", axis=0, tiled=True),
        lax.all_gather(kv_weight, "fsdp", axis=0, tiled=True),
    )
    vision, saved = encode(patches, ln_gain, full_qkv, full_out, tile_counts[0])
    back_weight = lax.all_gather(out_weight, "fsdp", axis=0, tiled=True)
    grad_qkv, grad_out = encode_grads(saved, back_weight, cotangent)
    shard_qkv, shard_out = (
        lax.psum_scatter(
            grad_qkv.astype(jnp.bfloat16), "fsdp", scatter_dimension=0, tiled=True
        ).astype(jnp.float32),
        lax.psum_scatter(
            grad_out.astype(jnp.bfloat16), "fsdp", scatter_dimension=0, tiled=True
        ).astype(jnp.float32),
    )
    sum_qkv, sum_out = lax.psum((shard_qkv, shard_out), "dp")
    counts_all = lax.all_gather(tile_counts, "fsdp", axis=0, tiled=True)
    key_total = groups * row_count
    local_kv = jnp.dot(vision, full_kv, preferred_element_type=jnp.float32).astype(jnp.bfloat16)
    local_kv = jnp.transpose(local_kv.reshape(row_count, KVH, 2 * HD), (1, 0, 2))
    outgoing = jnp.repeat(local_kv, groups // KVH, axis=0)
    arrived = lax.all_to_all(outgoing, "fsdp", split_axis=0, concat_axis=1, tiled=True)
    keys_values = arrived.reshape(key_total, 2 * HD)
    key_block = keys_values[:, :HD]
    value_block = keys_values[:, HD:]
    text_count = text_states.shape[0]
    queries = jnp.dot(text_states, query_weight, preferred_element_type=jnp.float32).astype(
        jnp.bfloat16
    )
    queries = queries.reshape(text_count, -1, HD)
    position = jnp.arange(key_total)
    image_of = position // row_count
    tile_of = position % row_count // PATCH
    key_live = tile_of < jnp.repeat(counts_all, row_count)
    allowed = key_live[None, :] & (image_of[None, :] < mask_ids[:, None])
    scores = jnp.einsum(
        "thd,kd->htk", queries, key_block, preferred_element_type=jnp.float32
    ) * HD ** (-0.5)
    scores = jnp.where(allowed[None], scores, NEG)
    row_top = jnp.max(scores, axis=-1, keepdims=True)
    weights = jnp.exp(scores - row_top)
    attn_low = (weights / jnp.sum(weights, axis=-1, keepdims=True)).astype(jnp.bfloat16)
    context = jnp.einsum("htk,kd->thd", attn_low, value_block, preferred_element_type=jnp.float32)
    context = context.astype(jnp.bfloat16).reshape(text_count, -1)
    partial_out = jnp.dot(context, output_weight, preferred_element_type=jnp.float32)
    attended = lax.psum_scatter(
        partial_out.astype(jnp.bfloat16), "fsdp", scatter_dimension=1, tiled=True
    ).astype(jnp.float32)
    col_width = attended.shape[1]
    text_cols = lax.dynamic_slice_in_dim(text_states, fsdp_index * col_width, col_width, 1)
    row_live = jnp.any(allowed, axis=-1) & (jnp.arange(text_count) < text_lengths[0])
    gate_tanh = jnp.tanh(gate_value[0])
    result = text_cols.astype(jnp.float32) + gate_tanh * jnp.where(row_live[:, None], attended, 0.0)
    return (sum_qkv, sum_out, result.astype(jnp.bfloat16))


def solution(mesh):
    placed = (
        P(("dp", "fsdp"), None),
        P(("dp", "fsdp"), None),
        P(("dp", "fsdp")),
        P(),
        P("fsdp", None),
        P("fsdp", None),
        P("dp", None),
        P("dp"),
        P("dp"),
        P(),
        P(None, "fsdp"),
        P("fsdp", None),
        P("fsdp", None),
    )
    return jax.shard_map(
        per_device,
        mesh=mesh,
        in_specs=placed,
        out_specs=(P("fsdp", None), P("fsdp", None), P("dp", "fsdp")),
        check_vma=False,
    )
```

profile of v0, /device:TPU:1, one launch (start us, length us, event | category | flops | bytes accessed | tf_op | source)
XLA Modules:
  0.0 610.5 jit_solution(10842560892253848947)
XLA Ops:
  11.2 1.2 fusion.30
  12.4 82.2 %all-gather.9.cloned.1.call-done = bf16[32,20,1280]{2,1,0:T(8,128)(2,1)} async-done(((bf16[1,20,1280]{2,1,0:T(8,128)(2,1)}), bf16[32,20,1280]{2,1,0:T(8,128)(2,1)}) %all-gather.9.cloned.1.call-update) | async-done | bytes 1638416 | tf_op jit(solution)/shard_map/all_gather | solution.py:106
  94.6 2.5 reshape.189
  97.9 85.4 %all-gather.5.cloned.1.call-done = bf16[1280,1920]{1,0:T(8,128)(2,1)} async-done(((bf16[40,1920]{1,0:T(8,128)(2,1)}), bf16[1280,1920]{1,0:T(8,128)(2,1)}) %all-gather.5.cloned.1.call-update) | async-done | bytes 4915216 | tf_op jit(solution)/shard_map/all_gather | solution.py:101
  183.3 3.4 convolution_convert_fusion.4
  187.3 1.2 fusion.86
  188.4 2.2 fusion.18
  190.6 2.2 fusion.19
  192.8 1.3 fusion.20
  195.3 3.8 convolution_convert_fusion.1
  200.4 73.1 %all-gather.7.cloned.1.call-done = bf16[1280,2048]{1,0:T(8,128)(2,1)} async-done(((bf16[40,2048]{1,0:T(8,128)(2,1)}), bf16[1280,2048]{1,0:T(8,128)(2,1)}) %all-gather.7.cloned.1.call-update) | async-done | bytes 5242896 | tf_op jit(solution)/shard_map/all_gather | solution.py:103
  273.5 3.7 convolution_convert_fusion.3
  277.5 1.5 broadcast_in_dim.86
  279.0 4.7 all-to-all-start
  285.1 56.9 %all-reduce = s32[32]{0:T(128)S(1)} all-reduce(s32[32]{0:T(128)S(1)} %dynamic-update-slice), channel_id=1, replica_groups=mesh['dp'=8,'fsdp'=32] {'fsdp'}, use_global_device_ids=true, to_apply=%add | all-reduce | flops 32 | bytes 256
  342.1 2.3 fusion.84
  344.5 2.9 fusion.22
  347.4 3.2 fusion.87
  350.6 4.0 fusion.21
  354.6 4.4 convolution_convert_fusion
  359.7 79.9 %fusion = bf16[24,1280]{1,0:T(8,128)(2,1)S(1)} fusion(bf16[640,1280]{1,0:T(8,128)(2,1)S(1)} %convolution_convert_fusion.2), kind=kCustom, calls=%all-reduce-scatter | all-reduce-scatter fusion | flops 983041 | bytes 1700864
  439.6 1.3 collective-permute-start.5
  441.5 1.9 collective-permute-start
  443.5 1.3 collective-permute-start.1
  444.8 2.9 collective-permute-start.2
  447.7 13.8 %collective-permute-start.3 = (bf16[24,1280]{1,0:T(8,128)(2,1)S(1)}, bf16[24,1280]{1,0:T(8,128)(2,1)S(1)}, u32[]{:S(2)}, u32[]{:S(2)}) collective-permute-start(bf16[24,1280]{1,0:T(8,128)(2,1)S(1)} %fusion), channel_id=1, source_target_pairs={{0,4},{1,5},{2,6},{3,7},{4,8},{5,9},{6,10},{7,11},{8,12},{9,13},{1... | collective-permute-start | bytes 184328
  461.5 2.2 collective-permute-start.4
  467.0 31.4 %all-reduce.8 = f32[40,1920]{1,0:T(8,128)} all-reduce(bf16[40,1920]{1,0:T(8,128)(2,1)} %reduce-scatter.9.cloned.1.call-done), channel_id=1, replica_groups=mesh['dp'=8,'fsdp'=32] {'dp'}, use_global_device_ids=true, to_apply=%region_6.7 | all-reduce | flops 76800 | bytes 460800 | tf_op jit(solution)/shard_map/psum | solution.py:116
  498.5 23.7 %reduce-scatter.7.cloned.1.call-done = bf16[128,256]{1,0:T(8,128)(2,1)} async-done(((bf16[128,8192]{1,0:T(8,128)(2,1)}), bf16[128,256]{1,0:T(8,128)(2,1)}) %reduce-scatter.7.cloned.1.call-update) | async-done | bytes 65552 | tf_op jit(solution)/shard_map/reduce_scatter | solution.py:146
  522.1 1.6 add_convert_fusion
  523.7 78.4 %all-reduce.7.cloned.1.call-done = f32[20,1280]{1,0:T(8,128)} async-done(((f32[20,1280]{1,0:T(8,128)}), f32[20,1280]{1,0:T(8,128)}) %all-reduce.7.cloned.1.call-update) | async-done | bytes 102416 | tf_op jit(solution)/shard_map/psum | solution.py:116
  602.1 1.6 copy.82
  (56 shorter events, 11.4 us)
Async XLA Ops:
  7.2 176.2 %copy-start = (bf16[128,1280]{1,0:T(8,128)(2,1)S(1)}, bf16[128,1280]{1,0:T(8,128)(2,1)}, u32[]{:S(2)}) copy-start(bf16[128,1280]{1,0:T(8,128)(2,1)} %param.13) | copy-start | bytes 983044
  7.2 89.9 %copy-start.2 = (bf16[128,1280]{1,0:T(8,128)(2,1)S(1)}, bf16[128,1280]{1,0:T(8,128)(2,1)}, u32[]{:S(2)}) copy-start(bf16[128,1280]{1,0:T(8,128)(2,1)} %param.14) | copy-start | bytes 983044
  7.2 176.2 %copy-start.3 = (f32[1280]{0:T(1024)S(1)}, f32[1280]{0:T(1024)}, u32[]{:S(2)}) copy-start(f32[1280]{0:T(1024)} %param.16) | copy-start | bytes 15364
  7.2 87.4 %all-gather.9.cloned.1.call-start = ((), (), s32[]{:S(2)}) async-start(), calls=%async_computation.7 | async-start | bytes 2027520 | tf_op jit(solution)/shard_map/all_gather | solution.py:106
  7.9 175.4 %all-gather.5.cloned.1.call-start = ((), (), s32[]{:S(2)}) async-start(), calls=%async_computation.3 | async-start | bytes 5068800 | tf_op jit(solution)/shard_map/all_gather | solution.py:101
  8.7 264.8 %all-gather.7.cloned.1.call-start = ((), (), s32[]{:S(2)}) async-start(), calls=%async_computation.5 | async-start | bytes 5406720 | tf_op jit(solution)/shard_map/all_gather | solution.py:103
  9.4 457.6 %reduce-scatter.9.cloned.1.call-start = ((), (), s32[]{:S(2)}) async-start(), calls=%async_computation.8 | async-start | bytes 5068800
  199.1 1.0 copy-start.6
  277.3 6.4 %copy-start.4 = (u32[256]{0:T(256)S(1)}, u32[256]{0:T(256)}, u32[]{:S(2)}) copy-start(u32[256]{0:T(256)} %constant.93) | copy-start | bytes 3076
  277.3 64.8 %copy-start.5 = (s32[128]{0:T(128)S(1)}, s32[128]{0:T(128)}, u32[]{:S(2)}) copy-start(s32[128]{0:T(128)} %param.20) | copy-start | bytes 1540
  277.3 67.1 %copy-start.1 = (bf16[128,8192]{1,0:T(8,128)(2,1)S(1)}, bf16[128,8192]{1,0:T(8,128)(2,1)}, u32[]{:S(2)}) copy-start(bf16[128,8192]{1,0:T(8,128)(2,1)} %param.19) | copy-start | bytes 6291460
  279.0 68.4 %all-to-all-start = ((bf16[32,128,256]{2,1,0:T(8,128)(2,1)}), bf16[32,128,256]{2,1,0:T(8,128)(2,1)}, u32[]{:S(2)}, u32[]{:S(2)}) async-start(bf16[32,128,256]{2,1,0:T(8,128)(2,1)} %bitcast.22), calls=%async_computation | async-start | bytes 4194304 | tf_op jit(solution)/shard_map/all_to_all | solution.py:122
  283.7 238.5 %reduce-scatter.7.cloned.1.call-start = ((), (), s32[]{:S(2)}) async-start(), calls=%async_computation.6 | async-start | bytes 2162688 | tf_op jit(solution)/shard_map/reduce_scatter | solution.py:146
  359.0 243.1 %all-reduce.7.cloned.1.call-start = ((), (), s32[]{:S(2)}) async-start(), calls=%async_computation.4 | async-start | bytes 245760 | tf_op jit(solution)/shard_map/psum | solution.py:116
  439.6 21.9 %collective-permute-start.5 = (bf16[4,1280]{1,0:T(4,128)(2,1)S(1)}, bf16[4,1280]{1,0:T(4,128)(2,1)S(1)}, u32[]{:S(2)}, u32[]{:S(2)}) collective-permute-start(bf16[4,1280]{1,0:T(4,128)(2,1)S(1)} %slice.25), channel_id=1, source_target_pairs={{0,6},{1,7},{2,8},{3,9},{4,10},{5,11},{6,12},{7,13},{8,14},{9,15},... | collective-permute-start | bytes 30728
  441.5 23.5 %collective-permute-start = (bf16[24,1280]{1,0:T(8,128)(2,1)S(1)}, bf16[24,1280]{1,0:T(8,128)(2,1)S(1)}, u32[]{:S(2)}, u32[]{:S(2)}) collective-permute-start(bf16[24,1280]{1,0:T(8,128)(2,1)S(1)} %fusion), channel_id=1, source_target_pairs={{0,1},{1,2},{2,3},{3,4},{4,5},{5,6},{6,7},{7,8},{8,9},{9,10},{10,1... | collective-permute-start | bytes 184328
  443.5 21.6 %collective-permute-start.1 = (bf16[24,1280]{1,0:T(8,128)(2,1)S(1)}, bf16[24,1280]{1,0:T(8,128)(2,1)S(1)}, u32[]{:S(2)}, u32[]{:S(2)}) collective-permute-start(bf16[24,1280]{1,0:T(8,128)(2,1)S(1)} %fusion), channel_id=1, source_target_pairs={{0,2},{1,3},{2,4},{3,5},{4,6},{5,7},{6,8},{7,9},{8,10},{9,11},{10,... | collective-permute-start | bytes 184328
  444.8 20.3 %collective-permute-start.2 = (bf16[24,1280]{1,0:T(8,128)(2,1)S(1)}, bf16[24,1280]{1,0:T(8,128)(2,1)S(1)}, u32[]{:S(2)}, u32[]{:S(2)}) collective-permute-start(bf16[24,1280]{1,0:T(8,128)(2,1)S(1)} %fusion), channel_id=1, source_target_pairs={{0,3},{1,4},{2,5},{3,6},{4,7},{5,8},{6,9},{7,10},{8,11},{9,12},{10... | collective-permute-start | bytes 184328
  447.7 17.4 %collective-permute-start.3 = (bf16[24,1280]{1,0:T(8,128)(2,1)S(1)}, bf16[24,1280]{1,0:T(8,128)(2,1)S(1)}, u32[]{:S(2)}, u32[]{:S(2)}) collective-permute-start(bf16[24,1280]{1,0:T(8,128)(2,1)S(1)} %fusion), channel_id=1, source_target_pairs={{0,4},{1,5},{2,6},{3,7},{4,8},{5,9},{6,10},{7,11},{8,12},{9,13},{1... | collective-permute-start | bytes 184328
  461.5 3.8 collective-permute-start.4
Sparse Core Ops, SparseCore 0:
  10.7 83.8 all-gather.8
  97.4 85.8 all-gather.4
  186.1 87.3 all-gather.6
  277.7 123.6 reduce-scatter.8
  405.4 116.6 reduce-scatter.6
  525.4 76.6 all-reduce.6
where the time goes:
time: 615 us; the launch traced here: 610 us
  waiting for transfers between devices  345 us (56%)
  blocking collectives  168 us (27%)
  matrix products  34 us (6%)
  starting transfers between devices  28.3 us (5%)
  between operations  17.1 us (3%)
  local copies, waits for them, and re-layouts  9.66 us (2%)
  other arithmetic  8.1 us (1%)
    unnamed x2, blocking collectives  137 us
    all_gather x1, waiting for transfers between devices, per_device(): lax.all_gather(qkv_weight, 'fsdp', axis=0, tiled=True)  85.4 us
    all_gather x1, waiting for transfers between devices, per_device(): back_weight = lax.all_gather(out_weight, 'fsdp', axis=0, tiled=True)  82.2 us
    psum x1, waiting for transfers between devices, per_device(): sum_qkv, sum_out = lax.psum((shard_qkv, shard_out), 'dp')  78.4 us
    all_gather x1, waiting for transfers between devices, per_device(): lax.all_gather(kv_weight, 'fsdp', axis=0, tiled=True)  73.1 us
    psum x1, blocking collectives, per_device(): sum_qkv, sum_out = lax.psum((shard_qkv, shard_out), 'dp')  31.4 us
    reduce_scatter x1, waiting for transfers between devices, per_device(): lax.psum_scatter(partial_out.astype(jnp.bfloat16), 'fsdp', scatter_dimens...  23.7 us
    unnamed x7, starting transfers between devices  23.4 us
  transfers between devices with their start and end apart: 13, of which 6 were waited for; matrix products, arithmetic and copies ran while one was open for 21% of the time, Pallas kernels for 0%

commit v1 on v0

--- a/solution.py
+++ b/solution.py
@@ -2,6 +2,8 @@
 import jax.numpy as jnp
 from jax import lax
 from jax.sharding import PartitionSpec as P
+from jax.experimental import pallas as pl
+from jax.experimental.pallas import tpu as pltpu
 
 EH = 8
 PATCH = 32
@@ -11,6 +13,193 @@
 
 EPS = 1e-05
 NEG = -1e30
+
+
+MESH = pl.DeviceIdType.MESH
+
+
+def place():
+    dp = lax.axis_index("dp")
+    f = lax.axis_index("fsdp")
+    x = lax.rem(dp, 4)
+    y = (f // 16) * 2 + dp // 4
+    z = lax.rem(f // 2, 8)
+    return x, y, z, lax.rem(f, 2)
+
+
+def device(x, y, z, core):
+    return (lax.rem(y, 2) * 4 + x, (y // 2) * 16 + z * 2 + core)
+
+
+def meet(peers):
+    barrier = pltpu.get_barrier_semaphore()
+    for peer in peers:
+        pl.semaphore_signal(barrier, inc=1, device_id=peer, device_id_type=MESH)
+    pl.semaphore_wait(barrier, len(peers))
+
+
+def remote(src, dst, send_sem, recv_sem, peer):
+    return pltpu.make_async_remote_copy(
+        src_ref=src, dst_ref=dst, send_sem=send_sem, recv_sem=recv_sem,
+        device_id=peer, device_id_type=MESH,
+    )
+
+
+def gather_kernel(a_ref, b_ref, a_full, b_full, local_sem, init_send, init_recv, z_send, z_recv,
+                  near_send, near_recv, far_send, far_recv, core_send, core_recv):
+    x, y, z, core = place()
+    y_hi = y // 2
+    partner = device(x, y, z, 1 - core)
+    y_mirror = 3 - y
+    spots = (y, x)
+    mirror_spots = (y_mirror, x)
+    shards = (a_ref, b_ref)
+    fulls = (a_full, b_full)
+
+    def along(t, step):
+        if t == 0:
+            return device(x, lax.rem(y + step + 4, 4), z, core)
+        return device(lax.rem(x + step + 4, 4), y, z, core)
+
+    def along_z(step):
+        return device(x, y, lax.rem(z + step + 8, 8), core)
+
+    meet([partner, device(x, y_mirror, z, 0), device(x, y_mirror, z, 1),
+          along_z(1), along_z(-1), along(0, 1), along(0, -1), along(1, 1), along(1, -1)])
+
+    def own_copy(t):
+        return pltpu.make_async_copy(
+            shards[t].at[spots[t]], fulls[t].at[spots[t], y_hi, z, core], local_sem.at[t])
+
+    def to_partner(t):
+        return remote(shards[t].at[spots[t]], fulls[t].at[spots[t], y_hi, z, core],
+                      init_send.at[t, 0], init_recv.at[t, core], partner)
+
+    def to_mirror(t):
+        return remote(shards[t].at[mirror_spots[t]], fulls[t].at[mirror_spots[t], y_hi, z, core],
+                      init_send.at[t, 1], init_recv.at[t, core], device(x, y_mirror, z, y_hi))
+
+    def from_core(t, other):
+        return remote(shards[t].at[spots[t]], fulls[t].at[spots[t], core, z, other],
+                      init_send.at[t, 0], init_recv.at[t, other], partner)
+
+    mine = core == y_hi
+    for t in range(2):
+        to_mirror(t).start()
+
+        @pl.when(mine)
+        def _(t=t):
+            own_copy(t).start()
+
+        @pl.when(jnp.logical_not(mine))
+        def _(t=t):
+            to_partner(t).start()
+
+    signs = (1, -1)
+
+    def unit_z(t, u):
+        d = (u + 1) // 2 if u % 2 else -(u // 2)
+        return lax.rem(z - signs[t] * d + 8, 8)
+
+    def unit(t, spot, u):
+        return fulls[t].at[spot, core, unit_z(t, u)]
+
+    def pass_on(t, spot, u):
+        src = unit(t, spot, u)
+        return remote(src, src, core_send.at[t], core_recv.at[t], partner)
+
+    def z_copy(t, u, u_next):
+        src = unit(t, spots[t], u)
+        step = signs[t] if u_next % 2 else -signs[t]
+        return remote(src, src, z_send.at[t], z_recv.at[t, u_next], along_z(step))
+
+    def near_copy(t, side, u):
+        src = unit(t, spots[t], u)
+        return remote(src, src, near_send.at[t], near_recv.at[t, side, u], along(t, 1 - 2 * side))
+
+    def far_copy(t, side, u):
+        spot = lax.rem(spots[t] + (3 if side == 0 else 1), 4)
+        src = fulls[t].at[spot, core, unit_z(t, u), side]
+        return remote(src, src, far_send.at[t], far_recv.at[t, side, u], along(t, 1 - 2 * side))
+
+    def near_arrival(t, side, u):
+        spot = lax.rem(spots[t] + (3 if side == 0 else 1), 4)
+        dst = unit(t, spot, u)
+        return remote(dst, dst, near_send.at[t], near_recv.at[t, side, u], partner)
+
+    def far_arrival(t, side, u):
+        spot = lax.rem(spots[t] + 2, 4)
+        dst = fulls[t].at[spot, core, unit_z(t, u), side]
+        return remote(dst, dst, far_send.at[t], far_recv.at[t, side, u], partner)
+
+    for u in range(10):
+        for t in range(2):
+            if u < 8:
+                if u == 0:
+                    @pl.when(mine)
+                    def _(t=t):
+                        own_copy(t).wait()
+                        from_core(t, 1 - core).wait_recv()
+
+                    @pl.when(jnp.logical_not(mine))
+                    def _(t=t):
+                        from_core(t, 0).wait_recv()
+                        from_core(t, 1).wait_recv()
+                    z_copy(t, 0, 1).start()
+                    z_copy(t, 0, 2).start()
+                else:
+                    z_copy(t, u, u).wait_recv()
+                    if u + 2 < 8:
+                        z_copy(t, u, u + 2).start()
+                near_copy(t, 0, u).start()
+                near_copy(t, 1, u).start()
+                pass_on(t, spots[t], u).start()
+        for t in range(2):
+            if 1 <= u < 9:
+                for side in range(2):
+                    near_arrival(t, side, u - 1).wait_recv()
+                    far_copy(t, side, u - 1).start()
+                for side in range(2):
+                    spot = lax.rem(spots[t] + (3 if side == 0 else 1), 4)
+                    pass_on(t, spot, u - 1).start()
+        for t in range(2):
+            if 2 <= u:
+                far_arrival(t, 0, u - 2).wait_recv()
+                far_arrival(t, 1, u - 2).wait_recv()
+                pass_on(t, lax.rem(spots[t] + 2, 4), u - 2).start()
+
+    for t in range(2):
+        to_mirror(t).wait_send()
+
+        @pl.when(jnp.logical_not(mine))
+        def _(t=t):
+            to_partner(t).wait_send()
+        seven = fulls[t].at[0, core, pl.ds(0, 7)]
+        two = fulls[t].at[pl.ds(0, 2), core]
+        one = fulls[t].at[0, core]
+        every = fulls[t].at[:, 1 - core]
+        remote(seven, seven, z_send.at[t], z_recv.at[t, 0], partner).wait_send()
+        remote(two, two, near_send.at[t], near_recv.at[t, 0, 0], partner).wait_send()
+        remote(one, one, far_send.at[t], far_recv.at[t, 0, 0], partner).wait_send()
+        remote(every, every, core_send.at[t], core_recv.at[t], partner).wait()
+
+
+def gather_weights(a, b):
+    dma = pltpu.SemaphoreType.DMA
+    any_space = pl.BlockSpec(memory_space=pl.ANY)
+    return pl.pallas_call(
+        gather_kernel,
+        out_shape=(jax.ShapeDtypeStruct((4, 2, 8, 2) + a.shape[1:], a.dtype),
+                   jax.ShapeDtypeStruct((4, 2, 8, 2) + b.shape[1:], b.dtype)),
+        in_specs=[any_space] * 2,
+        out_specs=[any_space] * 2,
+        scratch_shapes=[
+            dma((2,)), dma((2, 2)), dma((2, 2)), dma((2,)), dma((2, 8)),
+            dma((2,)), dma((2, 2, 8)), dma((2,)), dma((2, 2, 8)), dma((2,)), dma((2,)),
+        ],
+        compiler_params=pltpu.CompilerParams(collective_id=0, has_side_effects=True),
+        name="gather_weights",
+    )(a, b)
 
 
 def encode(patch_piece, ln_gain, qkv_weight, out_weight, tile_count):
@@ -22,13 +211,12 @@
     centred = inputs_f - row_mean
     spread = jnp.mean(centred * centred, axis=-1, keepdims=True)
     normed = (centred * lax.rsqrt(spread + EPS) * ln_gain).astype(jnp.bfloat16)
-    joined_qkv = jnp.dot(normed, qkv_weight, preferred_element_type=jnp.float32).astype(
-        jnp.bfloat16
-    )
-    joined_qkv = joined_qkv.reshape(row_count, 3, EH, head_size)
-    queries = joined_qkv[:, 0]
-    key_rows = joined_qkv[:, 1]
-    value_rows = joined_qkv[:, 2]
+    queries, key_rows, value_rows = (
+        jnp.dot(normed, qkv_weight[part], preferred_element_type=jnp.float32)
+        .astype(jnp.bfloat16)
+        .reshape(row_count, EH, head_size)
+        for part in range(3)
+    )
     live_rows = jnp.arange(row_count) // PATCH < tile_count
     scores = jnp.einsum(
         "qhd,khd->hqk", queries, key_rows, preferred_element_type=jnp.float32
@@ -97,14 +285,17 @@
     groups = lax.axis_size("fsdp")
     fsdp_index = lax.axis_index("fsdp")
     row_count = patches.shape[0]
-    full_qkv, full_out, full_kv = (
-        lax.all_gather(qkv_weight, "fsdp", axis=0, tiled=True),
-        lax.all_gather(out_weight, "fsdp", axis=0, tiled=True),
-        lax.all_gather(kv_weight, "fsdp", axis=0, tiled=True),
-    )
-    vision, saved = encode(patches, ln_gain, full_qkv, full_out, tile_counts[0])
-    back_weight = lax.all_gather(out_weight, "fsdp", axis=0, tiled=True)
-    grad_qkv, grad_out = encode_grads(saved, back_weight, cotangent)
+    out_halves = jnp.transpose(out_weight.reshape(-1, 2, 640), (1, 0, 2)).reshape(-1, 640)
+    joint = jnp.concatenate([qkv_weight, out_halves], axis=1)
+    joint = jnp.transpose(joint.reshape(-1, 4, 640), (1, 0, 2))
+    kv_parts = jnp.transpose(kv_weight.reshape(-1, 4, 512), (1, 0, 2))
+    joint_full, kv_full = gather_weights(joint, kv_parts)
+    joint_full = joint_full.reshape(4, 1280, 640)
+    kv_full = kv_full.reshape(4, 1280, 512)
+    full_out = joint_full[3].reshape(32, 2, 20, 640)
+    full_out = jnp.transpose(full_out, (0, 2, 1, 3)).reshape(640, 1280)
+    vision, saved = encode(patches, ln_gain, joint_full, full_out, tile_counts[0])
+    grad_qkv, grad_out = encode_grads(saved, full_out, cotangent)
     shard_qkv, shard_out = (
         lax.psum_scatter(
             grad_qkv.astype(jnp.bfloat16), "fsdp", scatter_dimension=0, tiled=True
@@ -116,7 +307,13 @@
     sum_qkv, sum_out = lax.psum((shard_qkv, shard_out), "dp")
     counts_all = lax.all_gather(tile_counts, "fsdp", axis=0, tiled=True)
     key_total = groups * row_count
-    local_kv = jnp.dot(vision, full_kv, preferred_element_type=jnp.float32).astype(jnp.bfloat16)
+    local_kv = jnp.concatenate(
+        [
+            jnp.dot(vision, kv_full[part], preferred_element_type=jnp.float32).astype(jnp.bfloat16)
+            for part in range(4)
+        ],
+        axis=1,
+    )
     local_kv = jnp.transpose(local_kv.reshape(row_count, KVH, 2 * HD), (1, 0, 2))
     outgoing = jnp.repeat(local_kv, groups // KVH, axis=0)
     arrived = lax.all_to_all(outgoing, "fsdp", split_axis=0, concat_axis=1, tiled=True)

time: 615 us -> 471 us (0.77)
  the two profiles are of different devices: /device:TPU:1 before, /device:TPU:8 now
where the time goes in v1:
time: 471 us; the launch traced here: 470 us
  blocking collectives  174 us (37%)
  waiting for transfers between devices  138 us (29%)
  Pallas kernels  46.8 us (10%)
  matrix products  32 us (7%)
  starting transfers between devices  28.8 us (6%)
  local copies, waits for them, and re-layouts  27 us (6%)
  between operations  18.7 us (4%)
  other arithmetic  5.18 us (1%)
    unnamed x2, blocking collectives  135 us
    unnamed x10, waiting for transfers between devices  133 us
    pallas_call x1, Pallas kernels, gather_weights(): pl.pallas_call(gather_kernel, out_shape=(jax.ShapeDtypeStruct((4, 2, 8, 2...  46.8 us
    psum x1, blocking collectives, per_device(): sum_qkv, sum_out = lax.psum((shard_qkv, shard_out), 'dp')  38.8 us
    unnamed x7, starting transfers between devices  21.6 us
  transfers between devices with their start and end apart: 10, of which 2 were waited for; matrix products, arithmetic and copies ran while one was open for 20% of the time, Pallas kernels for 0%

profile of v1, /device:TPU:8, one launch (start us, length us, event | category | flops | bytes accessed | tf_op | source)
XLA Modules:
  0.0 470.0 jit_solution(6672861928256754363)
XLA Ops:
  10.5 1.6 copy.102
  12.1 46.8 %gather_weights.1 = (bf16[4,2,8,2,40,640]{5,4,3,2,1,0:T(8,128)(2,1)}, bf16[4,2,8,2,40,512]{5,4,3,2,1,0:T(8,128)(2,1)}) custom-call(bf16[4,40,640]{2,1,0:T(8,128)(2,1)} %bitcast.161, bf16[4,40,512]{2,1,0:T(8,128)(2,1)} %bitcast.164), custom_call_target="tpu_custom_call" | custom-call | tf_op jit(solution)/shard_map/gather_weights/pallas_call | solution.py:190
  58.9 5.9 %fusion.82 = (bf16[1,2,8,2,40,640]{5,4,3,2,1,0:T(8,128)(2,1)}, bf16[1,2,8,2,40,640]{5,4,3,2,1,0:T(8,128)(2,1)}, bf16[1,2,8,2,40,640]{5,4,3,2,1,0:T(8,128)(2,1)}, bf16[1,2,8,2,40,640]{5,4,3,2,1,0:T(8,128)(2,1)}) fusion(bf16[4,2,8,2,40,640]{5,4,3,2,1,0:T(8,128)(2,1)} %get-tuple-element.5), kind=kLoop, calls=%fused_computation.118 | loop fusion | bytes 13107200 | tf_op jit(solution)/shard_map/slice | solution.py:215
  64.8 2.4 reshape.238
  67.2 1.3 copy.56
  70.7 2.0 convolution_convert_fusion.10
  73.5 1.9 convolution_convert_fusion.7
  76.2 4.5 fusion.83
  80.7 2.1 fusion.85
  82.8 1.5 convolution_convert_fusion.3
  87.2 1.5 broadcast_in_dim.86
  88.7 7.0 %all-to-all-start = ((bf16[32,128,256]{2,1,0:T(8,128)(2,1)}), bf16[32,128,256]{2,1,0:T(8,128)(2,1)}, u32[]{:S(2)}, u32[]{:S(2)}) async-start(bf16[32,128,256]{2,1,0:T(8,128)(2,1)} %bitcast.147), calls=%async_computation | async-start | bytes 4194304 | tf_op jit(solution)/shard_map/all_to_all | solution.py:319
  97.2 57.9 %all-reduce = s32[32]{0:T(128)S(1)} all-reduce(s32[32]{0:T(128)S(1)} %dynamic-update-slice), channel_id=1, replica_groups=mesh['dp'=8,'fsdp'=32] {'fsdp'}, use_global_device_ids=true, to_apply=%add | all-reduce | flops 32 | bytes 256
  155.2 1.4 fusion.81
  156.6 3.5 fusion.22
  160.2 3.1 fusion.86
  163.2 3.8 fusion.21
  167.1 4.3 convolution_convert_fusion
  173.5 1.6 fusion.19
  175.8 3.8 convolution_convert_fusion.1
  180.3 77.0 %fusion = bf16[24,1280]{1,0:T(8,128)(2,1)S(1)} fusion(bf16[640,1280]{1,0:T(8,128)(2,1)S(1)} %convolution_convert_fusion.2), kind=kCustom, calls=%all-reduce-scatter | all-reduce-scatter fusion | flops 983041 | bytes 1700864
  257.4 1.3 collective-permute-start.5
  258.7 1.3 collective-permute-start.4
  260.0 6.9 %collective-permute-start.3 = (bf16[24,1280]{1,0:T(8,128)(2,1)S(1)}, bf16[24,1280]{1,0:T(8,128)(2,1)S(1)}, u32[]{:S(2)}, u32[]{:S(2)}) collective-permute-start(bf16[24,1280]{1,0:T(8,128)(2,1)S(1)} %fusion), channel_id=1, source_target_pairs={{0,4},{1,5},{2,6},{3,7},{4,8},{5,9},{6,10},{7,11},{8,12},{9,13},{1... | collective-permute-start | bytes 184328
  266.9 2.9 collective-permute-start.2
  269.8 7.2 %collective-permute-start.1 = (bf16[24,1280]{1,0:T(8,128)(2,1)S(1)}, bf16[24,1280]{1,0:T(8,128)(2,1)S(1)}, u32[]{:S(2)}, u32[]{:S(2)}) collective-permute-start(bf16[24,1280]{1,0:T(8,128)(2,1)S(1)} %fusion), channel_id=1, source_target_pairs={{0,2},{1,3},{2,4},{3,5},{4,6},{5,7},{6,8},{7,9},{8,10},{9,11},{10,... | collective-permute-start | bytes 184328
  277.6 2.1 collective-permute-start
  282.8 5.2 %reduce-scatter.7.cloned.1.call-done = bf16[128,256]{1,0:T(8,128)(2,1)} async-done(((bf16[128,8192]{1,0:T(8,128)(2,1)}), bf16[128,256]{1,0:T(8,128)(2,1)}) %reduce-scatter.7.cloned.1.call-update) | async-done | bytes 65552 | tf_op jit(solution)/shard_map/reduce_scatter | solution.py:343
  288.0 1.6 add_convert_fusion
  289.6 132.7 %reduce-scatter.9.cloned.1.call-done = bf16[40,1920]{1,0:T(8,128)(2,1)} async-done(((bf16[1280,1920]{1,0:T(8,128)(2,1)}), bf16[40,1920]{1,0:T(8,128)(2,1)}) %reduce-scatter.9.cloned.1.call-update) | async-done | bytes 153616
  422.3 38.8 %all-reduce.8 = f32[40,1920]{1,0:T(8,128)} all-reduce(bf16[40,1920]{1,0:T(8,128)(2,1)} %reduce-scatter.9.cloned.1.call-done), channel_id=1, replica_groups=mesh['dp'=8,'fsdp'=32] {'dp'}, use_global_device_ids=true, to_apply=%region_6.7 | all-reduce | flops 76800 | bytes 460800 | tf_op jit(solution)/shard_map/psum | solution.py:307
  461.1 1.6 copy.111
  (81 shorter events, 15.0 us)
Async XLA Ops:
  68.5 1.1 copy-start
  68.5 1.6 copy-start.4
  68.5 1.5 copy-start.10
  70.7 10.0 %copy-start.7 = (bf16[128,640]{0,1:T(8,128)(2,1)}, bf16[128,640]{0,1:T(8,128)(2,1)S(1)}, u32[]{:S(2)}) copy-start(bf16[128,640]{0,1:T(8,128)(2,1)S(1)} %copy.54) | copy-start | bytes 491524
  82.8 2.0 copy-start.3
  84.3 1.3 copy-start.2
  84.8 1.4 copy-start.1
  88.7 7.1 %copy-start.11 = (u32[256]{0:T(256)S(1)}, u32[256]{0:T(256)}, u32[]{:S(2)}) copy-start(u32[256]{0:T(256)} %constant.93) | copy-start | bytes 3076
  88.7 66.5 %copy-start.12 = (s32[128]{0:T(128)S(1)}, s32[128]{0:T(128)}, u32[]{:S(2)}) copy-start(s32[128]{0:T(128)} %param.20) | copy-start | bytes 1540
  88.7 71.4 %all-to-all-start = ((bf16[32,128,256]{2,1,0:T(8,128)(2,1)}), bf16[32,128,256]{2,1,0:T(8,128)(2,1)}, u32[]{:S(2)}, u32[]{:S(2)}) async-start(bf16[32,128,256]{2,1,0:T(8,128)(2,1)} %bitcast.147), calls=%async_computation | async-start | bytes 4194304 | tf_op jit(solution)/shard_map/all_to_all | solution.py:319
  95.7 192.3 %reduce-scatter.7.cloned.1.call-start = ((), (), s32[]{:S(2)}) async-start(), calls=%async_computation.4 | async-start | bytes 2162688 | tf_op jit(solution)/shard_map/reduce_scatter | solution.py:343
  171.4 1.0 copy-start.5
  171.4 1.8 copy-start.6
  171.4 2.1 copy-start.8
  171.4 250.8 %reduce-scatter.9.cloned.1.call-start = ((), (), s32[]{:S(2)}) async-start(), calls=%async_computation.5 | async-start | bytes 5068800
  173.0 2.0 copy-start.9
  173.0 2.0 copy-start.13
  179.6 281.4 %all-reduce.7.cloned.1.call-start = ((), (), s32[]{:S(2)}) async-start(), calls=%async_computation.3 | async-start | bytes 245760 | tf_op jit(solution)/shard_map/psum | solution.py:307
  257.4 20.2 %collective-permute-start.5 = (bf16[4,1280]{1,0:T(4,128)(2,1)S(1)}, bf16[4,1280]{1,0:T(4,128)(2,1)S(1)}, u32[]{:S(2)}, u32[]{:S(2)}) collective-permute-start(bf16[4,1280]{1,0:T(4,128)(2,1)S(1)} %slice.50), channel_id=1, source_target_pairs={{0,6},{1,7},{2,8},{3,9},{4,10},{5,11},{6,12},{7,13},{8,14},{9,15},... | collective-permute-start | bytes 30728
  258.7 22.3 %collective-permute-start.4 = (bf16[24,1280]{1,0:T(8,128)(2,1)S(1)}, bf16[24,1280]{1,0:T(8,128)(2,1)S(1)}, u32[]{:S(2)}, u32[]{:S(2)}) collective-permute-start(bf16[24,1280]{1,0:T(8,128)(2,1)S(1)} %fusion), channel_id=1, source_target_pairs={{0,5},{1,6},{2,7},{3,8},{4,9},{5,10},{6,11},{7,12},{8,13},{9,14},{... | collective-permute-start | bytes 184328
  260.0 21.0 %collective-permute-start.3 = (bf16[24,1280]{1,0:T(8,128)(2,1)S(1)}, bf16[24,1280]{1,0:T(8,128)(2,1)S(1)}, u32[]{:S(2)}, u32[]{:S(2)}) collective-permute-start(bf16[24,1280]{1,0:T(8,128)(2,1)S(1)} %fusion), channel_id=1, source_target_pairs={{0,4},{1,5},{2,6},{3,7},{4,8},{5,9},{6,10},{7,11},{8,12},{9,13},{1... | collective-permute-start | bytes 184328
  266.9 14.1 %collective-permute-start.2 = (bf16[24,1280]{1,0:T(8,128)(2,1)S(1)}, bf16[24,1280]{1,0:T(8,128)(2,1)S(1)}, u32[]{:S(2)}, u32[]{:S(2)}) collective-permute-start(bf16[24,1280]{1,0:T(8,128)(2,1)S(1)} %fusion), channel_id=1, source_target_pairs={{0,3},{1,4},{2,5},{3,6},{4,7},{5,8},{6,9},{7,10},{8,11},{9,12},{10... | collective-permute-start | bytes 184328
  269.8 11.2 %collective-permute-start.1 = (bf16[24,1280]{1,0:T(8,128)(2,1)S(1)}, bf16[24,1280]{1,0:T(8,128)(2,1)S(1)}, u32[]{:S(2)}, u32[]{:S(2)}) collective-permute-start(bf16[24,1280]{1,0:T(8,128)(2,1)S(1)} %fusion), channel_id=1, source_target_pairs={{0,2},{1,3},{2,4},{3,5},{4,6},{5,7},{6,8},{7,9},{8,10},{9,11},{10,... | collective-permute-start | bytes 184328
  277.6 3.4 collective-permute-start
Sparse Core Ops, SparseCore 0:
  171.6 116.4 reduce-scatter.6
  293.0 129.2 reduce-scatter.8
Sparse Core Ops, SparseCore 1:
  282.9 72.3 all-reduce.6

commit v2 on v1

--- a/solution.py
+++ b/solution.py
@@ -200,6 +200,363 @@
         compiler_params=pltpu.CompilerParams(collective_id=0, has_side_effects=True),
         name="gather_weights",
     )(a, b)
+
+
+def reduce_peers():
+    x, y, z, core = place()
+    peers = [device(x, y, z, 1 - core)]
+    for step in range(1, 4):
+        for other in range(2):
+            peers.append(device(x, lax.rem(y + step, 4), z, other))
+            peers.append(device(lax.rem(x + step, 4), y, z, other))
+    for step in range(1, 8):
+        peers.append(device(x, y, lax.rem(z + step, 8), core))
+    return peers
+
+
+def reduce_steps(grads, out, from_core, chip_sum, from_near, plane_sum, from_z, from_cross, total,
+                 core_send, core_recv, near_send, near_recv, z_send, z_recv, cross_send, cross_recv,
+                 last_send, last_recv):
+    x, y, z, core = place()
+    y_hi = y // 2
+    partner = device(x, y, z, 1 - core)
+    spots = (y, x)
+    rows, width = out.shape[1:]
+
+    def along(axis, step):
+        if axis == 0:
+            return device(x, lax.rem(y + step, 4), z, core)
+        return device(lax.rem(x + step, 4), y, z, core)
+
+    def part(v, d):
+        return lax.rem(spots[v] + d, 4)
+
+    def core_copy(v, d):
+        return remote(grads.at[1 - core, v, part(v, d)], from_core.at[v, d],
+                      core_send.at[v, d], core_recv.at[v, d], partner)
+
+    def near_copy(v, d):
+        return remote(chip_sum.at[v, d - 1], from_near.at[v, d - 1],
+                      near_send.at[v, d - 1], near_recv.at[v, d - 1], along(v, d))
+
+    def z_copy(v, d):
+        return remote(plane_sum.at[v, lax.rem(z + d, 8)], from_z.at[v, d - 1],
+                      z_send.at[v, d - 1], z_recv.at[v, d - 1], device(x, y, lax.rem(z + d, 8), core))
+
+    def cross_copy(v, d):
+        slot = spots[1 - v]
+        return remote(from_cross.at[v, slot], from_cross.at[v, slot],
+                      cross_send.at[v, d - 1], cross_recv.at[v, d - 1], along(1 - v, d))
+
+    def cross_arrival(v, d):
+        slot = lax.rem(spots[1 - v] + 4 - d, 4)
+        return remote(from_cross.at[v, slot], from_cross.at[v, slot],
+                      cross_send.at[v, d - 1], cross_recv.at[v, d - 1], partner)
+
+    def last_copy(v, i):
+        peer = device(x, 2 * core + i, z, 0) if v == 0 else device(i, y, z, 1)
+        slot = spots[v]
+        return remote(total.at[v], out.at[slot], last_send.at[v, i], last_recv.at[slot], peer)
+
+    def last_self(v, i):
+        if v == 0:
+            return jnp.logical_and(2 * core + i == y, core == 0)
+        return jnp.logical_and(i == x, core == 1)
+
+    for d in (2, 1, 3, 0):
+        for v in range(2):
+            core_copy(v, d).start()
+    yield
+    for d in (2, 1, 3):
+        for v in range(2):
+            core_copy(v, d).wait_recv()
+
+            def add(k, carry, v=v, d=d):
+                chip_sum[v, d - 1, k] = (
+                    grads[core, v, part(v, d), k].astype(jnp.float32)
+                    + from_core[v, d, k].astype(jnp.float32)
+                ).astype(jnp.bfloat16)
+                return carry
+            lax.fori_loop(0, 8, add, 0)
+            near_copy(v, d).start()
+        yield
+    for v in range(2):
+        core_copy(v, 0).wait_recv()
+        for d in range(1, 4):
+            near_copy(v, d).wait_recv()
+
+        def add(k, carry, v=v):
+            sums = (grads[core, v, spots[v], k].astype(jnp.float32)
+                    + from_core[v, 0, k].astype(jnp.float32))
+            for d in range(3):
+                sums = sums + from_near[v, d, k].astype(jnp.float32)
+            plane_sum[v, k] = sums.astype(jnp.bfloat16)
+            return carry
+        lax.fori_loop(0, 8, add, 0)
+        for d in (4, 3, 5, 2, 6, 1, 7):
+            z_copy(v, d).start()
+        yield
+    for v in range(2):
+        for d in range(1, 8):
+            z_copy(v, d).wait_recv()
+        sums = plane_sum[v, z].astype(jnp.float32)
+        for d in range(7):
+            sums = sums + from_z[v, d].astype(jnp.float32)
+        from_cross[v, spots[1 - v]] = sums
+        for d in (2, 1, 3):
+            cross_copy(v, d).start()
+    yield
+    for v in range(2):
+        for d in range(1, 4):
+            cross_arrival(v, d).wait_recv()
+        total[v] = (from_cross[v, 0] + from_cross[v, 1]) + (from_cross[v, 2] + from_cross[v, 3])
+        for i in range(2 if v == 0 else 4):
+            active = True if v == 0 else y_hi == core
+
+            @pl.when(jnp.logical_and(active, jnp.logical_not(last_self(v, i))))
+            def _(v=v, i=i):
+                last_copy(v, i).start()
+
+            @pl.when(jnp.logical_and(active, last_self(v, i)))
+            def _(v=v):
+                out[spots[v]] = total[v]
+    yield
+    for j in range(4):
+        skip = jnp.where(core == 0, jnp.logical_and(j == y, y_hi == 0),
+                         jnp.logical_and(j == x, y_hi == 1))
+
+        @pl.when(jnp.logical_not(skip))
+        def _(j=j):
+            remote(out.at[j], out.at[j], last_send.at[0, 0], last_recv.at[j], partner).wait_recv()
+    for v in range(2):
+        for d in range(4):
+            core_copy(v, d).wait_send()
+        for d in range(1, 4):
+            near_copy(v, d).wait_send()
+            cross_copy(v, d).wait_send()
+        for d in range(1, 8):
+            z_copy(v, d).wait_send()
+        for i in range(2 if v == 0 else 4):
+            active = True if v == 0 else y_hi == core
+
+            @pl.when(jnp.logical_and(active, jnp.logical_not(last_self(v, i))))
+            def _(v=v, i=i):
+                last_copy(v, i).wait_send()
+
+
+def reduce_scratch():
+    dma = pltpu.SemaphoreType.DMA
+    block = (40, 640)
+    return [
+        pltpu.VMEM((2, 4, 8) + block, jnp.bfloat16),
+        pltpu.VMEM((2, 3, 8) + block, jnp.bfloat16),
+        pltpu.VMEM((2, 3, 8) + block, jnp.bfloat16),
+        pltpu.VMEM((2, 8) + block, jnp.bfloat16),
+        pltpu.VMEM((2, 7) + block, jnp.bfloat16),
+        pltpu.VMEM((2, 4) + block, jnp.float32),
+        pltpu.VMEM((2,) + block, jnp.float32),
+        dma((2, 4)), dma((2, 4)), dma((2, 3)), dma((2, 3)), dma((2, 7)), dma((2, 7)),
+        dma((2, 3)), dma((2, 3)), dma((2, 4)), dma((4,)),
+    ]
+
+
+def reduce_kernel(grads, out, *scratch):
+    meet(reduce_peers())
+    for _ in reduce_steps(grads, out, *scratch):
+        pass
+
+
+def reduce_grads(grads):
+    vmem = pl.BlockSpec(memory_space=pltpu.VMEM)
+    return pl.pallas_call(
+        reduce_kernel,
+        out_shape=jax.ShapeDtypeStruct((4, 40, 640), jnp.float32),
+        in_specs=[vmem],
+        out_specs=vmem,
+        scratch_shapes=reduce_scratch(),
+        compiler_params=pltpu.CompilerParams(
+            collective_id=1, has_side_effects=True, vmem_limit_bytes=56 * 2**20),
+        name="reduce_grads",
+    )(grads)
+
+
+def attended_peers():
+    x, y, z, core = place()
+    peers = [device(x, y, z, 1 - core), device(x, lax.rem(y + 2, 4), z, core)]
+    for step in range(1, 8):
+        peers.append(device(x, y, lax.rem(z + step, 8), core))
+    return peers
+
+
+def attended_steps(partial, out, from_core, chip_sum, from_y, group_sum, from_z,
+                   core_send, core_recv, y_send, y_recv, z_send, z_recv):
+    x, y, z, core = place()
+    y_hi = y // 2
+    partner = device(x, y, z, 1 - core)
+    across = device(x, lax.rem(y + 2, 4), z, core)
+    order = (4, 3, 5, 2, 6, 1, 7, 0)
+
+    def spot(d):
+        return lax.rem(z + d, 8)
+
+    def core_copy(half, d):
+        row = y_hi if half else 1 - y_hi
+        return remote(partial.at[row, spot(d), 1 - core], from_core.at[half, d],
+                      core_send.at[half, d], core_recv.at[half, d], partner)
+
+    def y_copy(d):
+        return remote(chip_sum.at[d], from_y.at[d], y_send.at[d], y_recv.at[d], across)
+
+    def z_copy(d):
+        return remote(group_sum.at[d], from_z.at[d], z_send.at[d], z_recv.at[d],
+                      device(x, y, spot(d), core))
+
+    for half in range(2):
+        for d in order:
+            core_copy(half, d).start()
+    yield
+    for d in order:
+        core_copy(0, d).wait_recv()
+        chip_sum[d] = (partial[1 - y_hi, spot(d), core].astype(jnp.float32)
+                       + from_core[0, d].astype(jnp.float32)).astype(jnp.bfloat16)
+        y_copy(d).start()
+    yield
+    for d in order:
+        core_copy(1, d).wait_recv()
+        y_copy(d).wait_recv()
+        sums = (partial[y_hi, spot(d), core].astype(jnp.float32)
+                + from_core[1, d].astype(jnp.float32) + from_y[d].astype(jnp.float32))
+        if d:
+            group_sum[d] = sums.astype(jnp.bfloat16)
+            z_copy(d).start()
+        else:
+            out[...] = sums
+    yield
+    sums = out[...]
+    for d in range(1, 8):
+        z_copy(d).wait_recv()
+        sums = sums + from_z[d].astype(jnp.float32)
+    out[...] = sums
+    for d in range(8):
+        core_copy(0, d).wait_send()
+        core_copy(1, d).wait_send()
+        y_copy(d).wait_send()
+        if d:
+            z_copy(d).wait_send()
+
+
+def attended_scratch():
+    dma = pltpu.SemaphoreType.DMA
+    block = (128, 256)
+    return [
+        pltpu.VMEM((2, 8) + block, jnp.bfloat16),
+        pltpu.VMEM((8,) + block, jnp.bfloat16),
+        pltpu.VMEM((8,) + block, jnp.bfloat16),
+        pltpu.VMEM((8,) + block, jnp.bfloat16),
+        pltpu.VMEM((8,) + block, jnp.bfloat16),
+        dma((2, 8)), dma((2, 8)), dma((8,)), dma((8,)), dma((8,)), dma((8,)),
+    ]
+
+
+def attended_kernel(partial, out, *scratch):
+    meet(attended_peers())
+    for _ in attended_steps(partial, out, *scratch):
+        pass
+
+
+def reduce_attended(partial):
+    vmem = pl.BlockSpec(memory_space=pltpu.VMEM)
+    return pl.pallas_call(
+        attended_kernel,
+        out_shape=jax.ShapeDtypeStruct((128, 256), jnp.float32),
+        in_specs=[vmem],
+        out_specs=vmem,
+        scratch_shapes=attended_scratch(),
+        compiler_params=pltpu.CompilerParams(
+            collective_id=2, has_side_effects=True, vmem_limit_bytes=56 * 2**20),
+        name="reduce_attended",
+    )(partial)
+
+
+def exchange_peers():
+    x, y, z, core = place()
+    peers = [device(x, y, z, 1 - core)]
+    for step in range(8):
+        for turn in range(2):
+            if step or turn:
+                peers.append(device(x, lax.rem(y + 2 * turn, 4), lax.rem(z + step, 8), core))
+    return peers
+
+
+ORDER = ((4, 1), (4, 0), (3, 1), (5, 1), (3, 0), (5, 0), (2, 1), (6, 1), (2, 0), (6, 0),
+         (1, 1), (7, 1), (1, 0), (7, 0), (0, 1), (0, 0))
+
+
+def exchange_steps(kv, arrived, local_sem, far_send, far_recv, core_send, core_recv):
+    x, y, z, core = place()
+    y_hi = y // 2
+    partner = device(x, y, z, 1 - core)
+
+    def far_copy(step, turn):
+        to_y = lax.rem(y + 2 * turn, 4)
+        to_z = lax.rem(z + step, 8)
+        head = (to_y // 2) * 4 + to_z // 2
+        return remote(kv.at[head], arrived.at[y_hi, z, core], far_send.at[step, turn],
+                      far_recv.at[step, turn], device(x, to_y, to_z, core))
+
+    def source(step, turn):
+        return arrived.at[lax.rem(y_hi + turn, 2), lax.rem(z + 8 - step, 8), core]
+
+    def pass_on(step, turn):
+        src = source(step, turn)
+        return remote(src, src, core_send.at[step, turn], core_recv.at[step, turn], partner)
+
+    own = pltpu.make_async_copy(kv.at[y_hi * 4 + z // 2], arrived.at[y_hi, z, core], local_sem)
+    own.start()
+    for step, turn in ORDER:
+        if step or turn:
+            far_copy(step, turn).start()
+    yield
+    for step, turn in reversed(ORDER):
+        if step or turn:
+            src = source(step, turn)
+            remote(src, src, far_send.at[step, turn], far_recv.at[step, turn], partner).wait_recv()
+        else:
+            own.wait()
+        pass_on(step, turn).start()
+    yield
+    for step, turn in reversed(ORDER):
+        dst = arrived.at[lax.rem(y_hi + turn, 2), lax.rem(z + 8 - step, 8), 1 - core]
+        remote(dst, dst, core_send.at[step, turn], core_recv.at[step, turn], partner).wait_recv()
+    for step, turn in ORDER:
+        pass_on(step, turn).wait_send()
+        if step or turn:
+            far_copy(step, turn).wait_send()
+
+
+def exchange_scratch():
+    dma = pltpu.SemaphoreType.DMA
+    return [dma(()), dma((8, 2)), dma((8, 2)), dma((8, 2)), dma((8, 2))]
+
+
+def exchange_kernel(kv, arrived, *scratch):
+    meet(exchange_peers())
+    for _ in exchange_steps(kv, arrived, *scratch):
+        pass
+
+
+def exchange_kv(kv):
+    vmem = pl.BlockSpec(memory_space=pltpu.VMEM)
+    return pl.pallas_call(
+        exchange_kernel,
+        out_shape=jax.ShapeDtypeStruct((2, 8, 2) + kv.shape[1:], kv.dtype),
+        in_specs=[vmem],
+        out_specs=vmem,
+        scratch_shapes=exchange_scratch(),
+        compiler_params=pltpu.CompilerParams(
+            collective_id=3, has_side_effects=True, vmem_limit_bytes=56 * 2**20),
+        name="exchange_kv",
+    )(kv)
 
 
 def encode(patch_piece, ln_gain, qkv_weight, out_weight, tile_count):
@@ -296,16 +653,13 @@
     full_out = jnp.transpose(full_out, (0, 2, 1, 3)).reshape(640, 1280)
     vision, saved = encode(patches, ln_gain, joint_full, full_out, tile_counts[0])
     grad_qkv, grad_out = encode_grads(saved, full_out, cotangent)
-    shard_qkv, shard_out = (
-        lax.psum_scatter(
-            grad_qkv.astype(jnp.bfloat16), "fsdp", scatter_dimension=0, tiled=True
-        ).astype(jnp.float32),
-        lax.psum_scatter(
-            grad_out.astype(jnp.bfloat16), "fsdp", scatter_dimension=0, tiled=True
-        ).astype(jnp.float32),
-    )
-    sum_qkv, sum_out = lax.psum((shard_qkv, shard_out), "dp")
-    counts_all = lax.all_gather(tile_counts, "fsdp", axis=0, tiled=True)
+    parts = grad_qkv.astype(jnp.bfloat16).reshape(2, 8, 2, 40, 3, 640)
+    parts = jnp.transpose(parts, (0, 2, 4, 1, 3, 5))
+    halves = grad_out.astype(jnp.bfloat16).reshape(2, 8, 2, 20, 2, 640)
+    halves = jnp.transpose(halves, (0, 2, 1, 4, 3, 5)).reshape(2, 2, 1, 8, 40, 640)
+    sums = reduce_grads(jnp.concatenate([parts, halves], axis=2))
+    sum_qkv = jnp.transpose(sums[:3], (1, 0, 2)).reshape(40, 1920)
+    sum_out = jnp.transpose(sums[3].reshape(2, 20, 640), (1, 0, 2)).reshape(20, 1280)
     key_total = groups * row_count
     local_kv = jnp.concatenate(
         [
@@ -315,9 +669,11 @@
         axis=1,
     )
     local_kv = jnp.transpose(local_kv.reshape(row_count, KVH, 2 * HD), (1, 0, 2))
-    outgoing = jnp.repeat(local_kv, groups // KVH, axis=0)
-    arrived = lax.all_to_all(outgoing, "fsdp", split_axis=0, concat_axis=1, tiled=True)
-    keys_values = arrived.reshape(key_total, 2 * HD)
+    count_rows = jnp.broadcast_to(tile_counts.astype(jnp.bfloat16)[:, None, None], (KVH, 16, 2 * HD))
+    arrived = exchange_kv(jnp.concatenate([local_kv, count_rows], axis=1))
+    arrived = arrived.reshape(groups, row_count + 16, 2 * HD)
+    counts_all = arrived[:, row_count, 0].astype(jnp.int32)
+    keys_values = arrived[:, :row_count].reshape(key_total, 2 * HD)
     key_block = keys_values[:, :HD]
     value_block = keys_values[:, HD:]
     text_count = text_states.shape[0]
@@ -340,9 +696,10 @@
     context = jnp.einsum("htk,kd->thd", attn_low, value_block, preferred_element_type=jnp.float32)
     context = context.astype(jnp.bfloat16).reshape(text_count, -1)
     partial_out = jnp.dot(context, output_weight, preferred_element_type=jnp.float32)
-    attended = lax.psum_scatter(
-        partial_out.astype(jnp.bfloat16), "fsdp", scatter_dimension=1, tiled=True
-    ).astype(jnp.float32)
+    blocks = jnp.transpose(
+        partial_out.astype(jnp.bfloat16).reshape(text_count, 2, 8, 2, 256), (1, 2, 3, 0, 4)
+    )
+    attended = reduce_attended(blocks)
     col_width = attended.shape[1]
     text_cols = lax.dynamic_slice_in_dim(text_states, fsdp_index * col_width, col_width, 1)
     row_live = jnp.any(allowed, axis=-1) & (jnp.arange(text_count) < text_lengths[0])

time: 471 us -> 270 us (0.57)
  the two profiles are of different devices: /device:TPU:8 before, /device:TPU:1 now
where the time goes in v2:
time: 270 us; the launch traced here: 268 us
  Pallas kernels  174 us (64%)
  local copies, waits for them, and re-layouts  53.2 us (20%)
  matrix products  27.7 us (10%)
  other arithmetic  9.93 us (4%)
  between operations  3.06 us (1%)
    pallas_call x1, Pallas kernels, reduce_grads(): pl.pallas_call(reduce_kernel, out_shape=jax.ShapeDtypeStruct((4, 40, 640)...  62 us
    pallas_call x1, Pallas kernels, gather_weights(): pl.pallas_call(gather_kernel, out_shape=(jax.ShapeDtypeStruct((4, 2, 8, 2...  50.1 us
    pallas_call x1, Pallas kernels, exchange_kv(): pl.pallas_call(exchange_kernel, out_shape=jax.ShapeDtypeStruct((2, 8, 2)...  37.4 us
    pallas_call x1, Pallas kernels, reduce_attended(): pl.pallas_call(attended_kernel, out_shape=jax.ShapeDtypeStruct((128, 256)...  24.9 us
    reshape x2, local copies, waits for them, and re-layouts, per_device(): parts = grad_qkv.astype(jnp.bfloat16).reshape(2, 8, 2, 40, 3, 640)  17.2 us

profile of v2, /device:TPU:1, one launch (start us, length us, event | category | flops | bytes accessed | tf_op | source)
XLA Modules:
  0.0 268.3 jit_solution(8552393437274867823)
XLA Ops:
  0.6 1.1 convert_reduce_fusion
  1.7 1.2 fusion.28
  3.0 0.9 reshape.232
  3.9 0.9 pad_maximum_fusion.3
  5.5 1.6 copy.125
  7.1 50.1 %gather_weights.1 = (bf16[4,2,8,2,40,640]{5,4,3,2,1,0:T(8,128)(2,1)}, bf16[4,2,8,2,40,512]{5,4,3,2,1,0:T(8,128)(2,1)}) custom-call(bf16[4,40,640]{2,1,0:T(8,128)(2,1)} %bitcast.182, bf16[4,40,512]{2,1,0:T(8,128)(2,1)} %bitcast.185), custom_call_target="tpu_custom_call" | custom-call | tf_op jit(solution)/shard_map/gather_weights/pallas_call | solution.py:190
  57.2 5.4 %fusion.81 = (bf16[1,2,8,2,40,640]{5,4,3,2,1,0:T(8,128)(2,1)}, bf16[1,2,8,2,40,640]{5,4,3,2,1,0:T(8,128)(2,1)S(1)}, bf16[1,2,8,2,40,640]{5,4,3,2,1,0:T(8,128)(2,1)}, bf16[1,2,8,2,40,640]{5,4,3,2,1,0:T(8,128)(2,1)S(1)}) fusion(bf16[4,2,8,2,40,640]{5,4,3,2,1,0:T(8,128)(2,1)} %get-tuple-element.5), kind=kLoop, calls=%fused_computation.121 | loop fusion | bytes 13107200 | tf_op jit(solution)/shard_map/slice | solution.py:652
  63.3 2.0 convolution_convert_fusion.9
  67.4 2.6 reshape.257
  70.0 1.3 copy.66
  72.0 3.1 %fusion.82 = (bf16[1,2,8,2,40,512]{5,4,3,2,1,0:T(8,128)(2,1)S(1)}, bf16[1,2,8,2,40,512]{5,4,3,2,1,0:T(8,128)(2,1)S(1)}, bf16[1,2,8,2,40,512]{5,4,3,2,1,0:T(8,128)(2,1)S(1)}, bf16[1,2,8,2,40,512]{5,4,3,2,1,0:T(8,128)(2,1)S(1)}) fusion(bf16[4,2,8,2,40,512]{5,4,3,2,1,0:T(8,128)(2,1)} %get-tuple-element.6), kind=kLoop, calls=%fused_computation.122 | loop fusion | bytes 10485760 | tf_op jit(solution)/shard_map/slice | solution.py:666
  77.0 0.9 concatenate.15.kv
  77.9 37.4 %exchange_kv.1 = bf16[2,8,2,144,256]{4,3,2,1,0:T(8,128)(2,1)} custom-call(bf16[8,144,256]{2,1,0:T(8,128)(2,1)} %concatenate.15.kv), custom_call_target="tpu_custom_call" | custom-call | tf_op jit(solution)/shard_map/exchange_kv/pallas_call | solution.py:550
  115.3 3.1 %slice.65 = bf16[32,128,256]{2,1,0:T(8,128)(2,1)} slice(bf16[32,144,256]{2,1,0:T(8,128)(2,1)} %bitcast.162), slice={[0:32], [0:128], [0:256]} | slice | bytes 4194304 | tf_op jit(solution)/shard_map/slice | solution.py:676
  119.5 1.4 fusion.80
  120.9 3.5 %fusion.21 = bf16[16,2,8,128]{3,2,1,0:T(8,128)(2,1)S(1)} fusion(bf16[128,8192]{1,0:T(8,128)(2,1)} %param.19, bf16[8192,256]{1,0:T(8,128)(2,1)} %param.23), kind=kOutput, calls=%fused_computation.44 | convolution fusion | flops 536903680 | bytes 6356992 | tf_op jit(solution)/shard_map/dot_general | solution.py:680
  124.5 3.1 %fusion.84 = f32[2,128]{1,0:T(2,128)S(1)} fusion(pred[128,4096]{0,1:T(8,128)(4,1)S(1)} %get-tuple-element.16, bf16[4096,256]{1,0:T(8,128)(2,1)} %bitcast.173, bf16[16,2,8,128]{3,2,1,0:T(8,128)(2,1)S(1)} %fusion.21), kind=kOutput, calls=%fused_computation.124 | convolution fusion | flops 272633856 | bytes 1639424 | tf_op jit(solution)/shard_map/sub | solution.py:694
  127.6 3.8 %fusion.20 = bf16[128,2,128]{2,0,1:T(8,128)(2,1)S(1)} fusion(f32[2,128]{1,0:T(2,128)S(1)} %fusion.84, bf16[4096,256]{1,0:T(8,128)(2,1)} %bitcast.174, pred[128,4096]{0,1:T(8,128)(4,1)S(1)} %get-tuple-element.16, bf16[16,2,8,128]{3,2,1,0:T(8,128)(2,1)S(1)} %fusion.21), kind=kOutput, calls=%fused_computation.42 | convolution fusion | flops 542150912 | bytes 2753536 | tf_op jit(solution)/shard_map/htk,kd->thd/dot_general | solution.py:696
  131.4 4.2 %convolution_convert_fusion = bf16[128,8192]{1,0:T(8,128)(2,1)} fusion(bf16[128,256]{0,1:T(8,128)(2,1)S(1)} %bitcast.200, bf16[256,8192]{1,0:T(8,128)(2,1)} %param.25), kind=kOutput, calls=%fused_computation.3 | convolution fusion | flops 537919488 | bytes 6356992 | tf_op jit(solution)/shard_map/dot_general | solution.py:698
  135.6 4.1 %copy.84 = bf16[128,8192]{0,1:T(8,128)(2,1)} copy(bf16[128,8192]{1,0:T(8,128)(2,1)} %convolution_convert_fusion) | data formatting | bytes 4194304 | tf_op jit(solution)/shard_map/convert_element_type | solution.py:700
  139.7 3.9 %copy.85 = bf16[128,2,8,2,256]{4,0,3,2,1:T(8,128)(2,1)} copy(bf16[128,2,8,2,256]{0,4,3,2,1:T(8,128)(2,1)} %bitcast.164) | data formatting | bytes 4194304 | tf_op jit(solution)/shard_map/reshape | solution.py:700
  143.7 24.9 %reduce_attended.1 = f32[128,256]{1,0:T(8,128)} custom-call(bf16[2,8,2,128,256]{4,3,2,1,0:T(8,128)(2,1)} %bitcast.165), custom_call_target="tpu_custom_call" | custom-call | tf_op jit(solution)/shard_map/reduce_attended/pallas_call | solution.py:469
  169.9 1.6 add_convert_fusion
  172.7 1.6 fusion.17
  175.0 3.9 %convolution_convert_fusion.1 = bf16[1280,1920]{1,0:T(8,128)(2,1)} fusion(bf16[128,1920]{0,1:T(8,128)(2,1)S(1)} %bitcast.177, bf16[128,1280]{1,0:T(8,128)(2,1)S(1)} %copy-done.1, f32[1280]{0:T(1024)S(1)} %copy-done.8, f32[128]{0:T(128)S(1)} %add_rsqrt_fusion, f32[128]{0:T(128)S(1)} %broadcast_multiply_fusion), kind=kOutput, calls=%fused_computation.4 | convolution fusion | flops 632422400 | bytes 5740544 | tf_op jit(solution)/shard_map/dot_general | solution.py:621
  178.9 11.1 %reshape.241 = bf16[2,8,2,40,3,640]{5,4,3,2,1,0:T(4,128)(2,1)} reshape(bf16[1280,1920]{1,0:T(8,128)(2,1)} %convolution_convert_fusion.1) | data formatting | bytes 9830400 | tf_op jit(solution)/shard_map/reshape | solution.py:656
  190.0 6.1 %copy.123 = bf16[2,8,2,40,3,640]{5,3,1,4,2,0:T(8,128)(2,1)} copy(bf16[2,8,2,40,3,640]{5,4,3,2,1,0:T(4,128)(2,1)} %reshape.241) | data formatting | bytes 9830400 | tf_op jit(solution)/shard_map/reshape | solution.py:656
  197.7 1.8 copy-done
  199.5 3.4 %pad_maximum_fusion.grads = bf16[2,2,4,8,40,640]{5,4,3,2,1,0:T(8,128)(2,1)} fusion(bf16[2,2,1,8,40,640]{5,4,3,2,1,0:T(8,128)(2,1)S(1)} %copy.75, bf16[2,2,3,8,40,640]{5,4,3,2,1,0:T(8,128)(2,1)S(1)} %bitcast.159), kind=kLoop, calls=%fused_computation.5 | loop fusion | flops 3276800 | bytes 13107200 | tf_op jit(solution)/shard_map/concatenate | solution.py:660
  203.0 62.0 %reduce_grads.1 = f32[4,40,640]{2,1,0:T(8,128)} custom-call(bf16[2,2,4,8,40,640]{5,4,3,2,1,0:T(8,128)(2,1)} %pad_maximum_fusion.grads), custom_call_target="tpu_custom_call" | custom-call | tf_op jit(solution)/shard_map/reduce_grads/pallas_call | solution.py:371
  264.9 1.0 slice_bitcast_fusion.10
  266.7 0.9 slice.55
  (66 shorter events, 11.4 us)
Async XLA Ops:
  57.2 5.4 %copy-start.1 = (bf16[128,1280]{1,0:T(8,128)(2,1)S(1)}, bf16[128,1280]{1,0:T(8,128)(2,1)}, u32[]{:S(2)}) copy-start(bf16[128,1280]{1,0:T(8,128)(2,1)} %param.13) | copy-start | bytes 983044
  57.2 5.4 %copy-start.8 = (f32[1280]{0:T(1024)S(1)}, f32[1280]{0:T(1024)}, u32[]{:S(2)}) copy-start(f32[1280]{0:T(1024)} %param.16) | copy-start | bytes 15364
  63.3 3.7 %copy-start.5 = (bf16[128,640]{0,1:T(8,128)(2,1)}, bf16[128,640]{0,1:T(8,128)(2,1)S(1)}, u32[]{:S(2)}) copy-start(bf16[128,640]{0,1:T(8,128)(2,1)S(1)} %copy.63) | copy-start | bytes 491524
  65.4 2.0 copy-start.6
  66.5 0.9 copy-start.10
  67.1 2.8 %copy-start.3 = (bf16[128,640]{0,1:T(8,128)(2,1)}, bf16[128,640]{0,1:T(8,128)(2,1)S(1)}, u32[]{:S(2)}) copy-start(bf16[128,640]{0,1:T(8,128)(2,1)S(1)} %copy.68) | copy-start | bytes 491524
  115.3 4.2 %copy-start.9 = (s32[128]{0:T(128)S(1)}, s32[128]{0:T(128)}, u32[]{:S(2)}) copy-start(s32[128]{0:T(128)} %param.20) | copy-start | bytes 1540
  143.7 27.9 %copy-start.2 = (bf16[128,1280]{1,0:T(8,128)(2,1)S(1)}, bf16[128,1280]{1,0:T(8,128)(2,1)}, u32[]{:S(2)}) copy-start(bf16[128,1280]{1,0:T(8,128)(2,1)} %param.14) | copy-start | bytes 983044
  143.7 28.7 %copy-start.4 = (bf16[128,640]{0,1:T(8,128)(2,1)S(1)}, bf16[128,640]{0,1:T(8,128)(2,1)}, u32[]{:S(2)}) copy-start(bf16[128,640]{0,1:T(8,128)(2,1)} %copy-done.3) | copy-start | bytes 491524
  172.2 2.1 copy-start.7
  172.2 2.0 copy-start.11
  197.1 2.4 copy-start

commit v3 on v2

v3 whole, which is shorter than its diff:
```python
import jax
import jax.numpy as jnp
import numpy as np
from jax import lax
from jax.sharding import PartitionSpec as P
from jax.experimental import pallas as pl
from jax.experimental.pallas import tpu as pltpu

EH = 8
EHD = 80
PATCH = 32
HD = 128
KVH = 8
LAG = 3

EPS = 1e-05
NEG = -1e30

MESH = pl.DeviceIdType.MESH


def place():
    dp = lax.axis_index("dp")
    f = lax.axis_index("fsdp")
    x = lax.rem(dp, 4)
    y = (f // 16) * 2 + dp // 4
    z = lax.rem(f // 2, 8)
    return x, y, z, lax.rem(f, 2)


def device(x, y, z, core):
    return (lax.rem(y, 2) * 4 + x, (y // 2) * 16 + z * 2 + core)


def meet(peers):
    barrier = pltpu.get_barrier_semaphore()
    for peer in peers:
        pl.semaphore_signal(barrier, inc=1, device_id=peer, device_id_type=MESH)
    pl.semaphore_wait(barrier, len(peers))


def remote(src, dst, send_sem, recv_sem, peer):
    return pltpu.make_async_remote_copy(
        src_ref=src, dst_ref=dst, send_sem=send_sem, recv_sem=recv_sem,
        device_id=peer, device_id_type=MESH,
    )


def gather_scratch():
    dma = pltpu.SemaphoreType.DMA
    return [
        dma((2, 2)), dma((2, 2)), dma((2, 8)), dma((2, 8)),
        dma((2, 2, 8)), dma((2, 2, 8)), dma((2, 8)), dma((2, 8)), dma((2, 8)), dma((2, 8)),
    ]


def gather_peers():
    x, y, z, core = place()
    peers = [device(x, y, z, 1 - core), device(x, 3 - y, z, 0), device(x, 3 - y, z, 1)]
    for step in (1, 3):
        peers.append(device(x, lax.rem(y + step, 4), z, core))
        peers.append(device(lax.rem(x + step, 4), y, z, core))
    for step in (1, 7):
        peers.append(device(x, y, lax.rem(z + step, 8), core))
    return peers


def gather_steps(t, shard, full, pair, init_send, init_recv, z_send, z_recv, near_send, near_recv,
                 far_send, far_recv, core_send, core_recv):
    x, y, z, core = place()
    y_hi = y // 2
    partner = device(x, y, z, 1 - core)
    width = pair.shape[2]
    sign = 1 - 2 * t
    mine = core == y_hi

    def turned(where):
        return lax.rem(where + t, 2)

    def spot_at(where, my_y):
        return my_y + turned(where) * (x - my_y)

    def columns(spot):
        return shard.at[:, pl.ds(pl.multiple_of(spot * width, 128), width)]

    def unit_z(u):
        d = (u + 1) // 2 if u % 2 else -(u // 2)
        return lax.rem(z - sign * d + 8, 8)

    def along_z(step):
        return device(x, y, lax.rem(z + step + 8, 8), core)

    def along(where, step):
        by_x = turned(where)
        return device(lax.rem(x + by_x * step + 4, 4), lax.rem(y + (1 - by_x) * step + 4, 4), z, core)

    def unit(u, d):
        where = unit_z(u)
        return full.at[lax.rem(spot_at(where, y) + d, 4), core, where]

    def to_partner():
        return remote(columns(spot_at(z, y)), pair.at[core], init_send.at[t, 0],
                      init_recv.at[t, core], partner)

    def to_mirror():
        return remote(columns(spot_at(z, 3 - y)), pair.at[core], init_send.at[t, 1],
                      init_recv.at[t, core], device(x, 3 - y, z, y_hi))

    def own_copy():
        return pltpu.make_async_copy(columns(spot_at(z, y)), pair.at[core], init_send.at[t, 0])

    def from_core(other):
        return remote(pair.at[other], pair.at[other], init_send.at[t, 0], init_recv.at[t, other], partner)

    def z_copy(u, u_next):
        src = unit(u, 0)
        step = sign if u_next % 2 else -sign
        return remote(src, src, z_send.at[t, u_next], z_recv.at[t, u_next], along_z(step))

    def near_copy(side, u):
        src = unit(u, 0)
        return remote(src, src, near_send.at[t, side, u], near_recv.at[t, side, u],
                      along(unit_z(u), 1 - 2 * side))

    def near_arrival(side, u):
        dst = unit(u, 3 - 2 * side)
        return remote(dst, dst, near_send.at[t, side, u], near_recv.at[t, side, u], partner)

    def far_copy(u):
        where = unit_z(u)
        back = lax.rem(where // 2, 2)
        src = unit(u, 3 - 2 * back)
        return remote(src, src, far_send.at[t, u], far_recv.at[t, u], along(where, 1 - 2 * back))

    def far_arrival(u):
        dst = unit(u, 2)
        return remote(dst, dst, far_send.at[t, u], far_recv.at[t, u], partner)

    def pass_on(u):
        src = full.at[:, core, unit_z(u)]
        return remote(src, src, core_send.at[t, u], core_recv.at[t, u], partner)

    def passed(u):
        dst = full.at[:, 1 - core, unit_z(u)]
        return remote(dst, dst, core_send.at[t, u], core_recv.at[t, u], partner)

    to_mirror().start()

    @pl.when(mine)
    def _():
        own_copy().start()

    @pl.when(jnp.logical_not(mine))
    def _():
        to_partner().start()
    yield
    for u in range(10):
        if u == 0:
            @pl.when(mine)
            def _():
                own_copy().wait()
                from_core(1 - core).wait_recv()

            @pl.when(jnp.logical_not(mine))
            def _():
                from_core(0).wait_recv()
                from_core(1).wait_recv()
            both = jnp.concatenate([pair[0].astype(jnp.float32), pair[1].astype(jnp.float32)], axis=0)
            full[spot_at(z, y), core, z] = both.astype(jnp.bfloat16)
            z_copy(0, 1).start()
            z_copy(0, 2).start()
        elif u < 8:
            z_copy(u, u).wait_recv()
            if u + 2 < 8:
                z_copy(u, u + 2).start()
        if u < 8:
            near_copy(0, u).start()
            near_copy(1, u).start()
        if 1 <= u < 9:
            for side in range(2):
                near_arrival(side, u - 1).wait_recv()
            far_copy(u - 1).start()
        if 2 <= u:
            far_arrival(u - 2).wait_recv()
            pass_on(u - 2).start()
        yield
    to_mirror().wait_send()

    @pl.when(jnp.logical_not(mine))
    def _():
        to_partner().wait_send()
    for u in range(8):
        passed(u).wait_recv()
        pass_on(u).wait_send()
        if u:
            z_copy(0, u).wait_send()
        near_copy(0, u).wait_send()
        near_copy(1, u).wait_send()
        far_copy(u).wait_send()
    yield


def dot(a, b, over=((1,), (0,))):
    return lax.dot_general(a, b, (over, ((), ())), preferred_element_type=jnp.float32)


def head_stack(rows, head_mask):
    return jnp.concatenate([rows * head_mask[h:h + 1] for h in range(EH)], axis=0)


def head_pick(stack, head_mask):
    rows = stack.shape[0] // EH
    total = jnp.zeros((rows, stack.shape[1]), jnp.float32)
    for h in range(EH):
        total = total + stack[h * rows:(h + 1) * rows] * head_mask[h:h + 1].astype(jnp.float32)
    return total


def encode_kernel(count_ref, patches, gain, joint, kv_shard, text, query_weight, head_mask, pick,
                  half_mask, kv_out, queries_out, normed_out, qkv_out, probs_out, spread_out, out_weight,
                  joint_full, kv_full, joint_pair, kv_pair, text_in, query_in, local_sem, *sems):
    meet(gather_peers())
    first = gather_steps(0, joint, joint_full, joint_pair, *sems)
    second = gather_steps(1, kv_shard, kv_full, kv_pair, *sems)
    next(first)
    next(second)
    load_text = pltpu.make_async_copy(text, text_in, local_sem.at[0])
    load_query = pltpu.make_async_copy(query_weight, query_in, local_sem.at[1])
    load_text.start()
    load_query.start()

    next(first)
    inputs = patches[...].astype(jnp.float32)
    centred = inputs - jnp.mean(inputs, axis=-1, keepdims=True)
    spread = jnp.mean(centred * centred, axis=-1, keepdims=True)
    normed = (centred * lax.rsqrt(spread + EPS) * gain[...]).astype(jnp.bfloat16)
    normed_out[...] = normed
    next(first)
    load_text.wait()
    load_query.wait()
    queries = jnp.zeros(queries_out.shape, jnp.float32)
    for step in range(8):
        queries = queries + dot(text_in[:, step * 1024:(step + 1) * 1024],
                                query_in[step * 1024:(step + 1) * 1024, :])
        next(first)
        if step >= LAG:
            next(second)
    queries_out[...] = queries.astype(jnp.bfloat16)
    next(first)

    masks = head_mask[...]
    rows = inputs.shape[0]
    next(second)
    query = dot(normed_out[...], joint_full[0].reshape(1280, 640)).astype(jnp.bfloat16)
    qkv_out[0] = query
    next(second)
    key = dot(normed_out[...], joint_full[1].reshape(1280, 640)).astype(jnp.bfloat16)
    qkv_out[1] = key
    next(second)
    value = dot(normed_out[...], joint_full[2].reshape(1280, 640)).astype(jnp.bfloat16)
    qkv_out[2] = value
    out_weight[...] = joint_full[3].reshape(1280, 640)
    next(second)
    live_key = lax.broadcasted_iota(jnp.int32, (1, rows), 1) < count_ref[0] * PATCH
    live_row = lax.broadcasted_iota(jnp.int32, (rows, 1), 0) < count_ref[0] * PATCH
    scores = dot(head_stack(query, masks), key, ((1,), (1,))) * EHD ** (-0.5)
    scores = jnp.where(live_key, scores, NEG)
    weights = jnp.exp(scores - jnp.max(scores, axis=-1, keepdims=True))
    probs = weights / jnp.sum(weights, axis=-1, keepdims=True)
    probs_out[...] = probs
    next(second)
    context = head_pick(dot(probs.astype(jnp.bfloat16), value), masks).astype(jnp.bfloat16)
    both = dot(context, pick[...], ((1,), (1,))).astype(jnp.bfloat16)
    halves = jnp.concatenate([both * half_mask[0:1], both * half_mask[1:2]], axis=0)
    spread_out[...] = halves
    branch = dot(halves, out_weight[...])
    branch = jnp.concatenate([branch[:rows], branch[rows:]], axis=1)
    vision = jnp.where(live_row, patches[...].astype(jnp.float32) + branch, 0.0).astype(jnp.bfloat16)
    for _ in second:
        pass
    for part in range(4):
        piece = dot(vision, kv_full[part].reshape(1280, 512)).astype(jnp.bfloat16)
        for side in range(2):
            kv_out[2 * part + side, pl.ds(0, rows), :] = piece[:, side * 256:(side + 1) * 256]
    number = jnp.full((KVH, 16, 256), count_ref[0].astype(jnp.float32)).astype(jnp.bfloat16)
    kv_out[:, pl.ds(rows, 16), :] = number


def encode(count, patches, gain, joint, kv_shard, text, query_weight, head_mask, pick, half_mask):
    dma = pltpu.SemaphoreType.DMA
    vmem = pl.BlockSpec(memory_space=pltpu.VMEM)
    any_space = pl.BlockSpec(memory_space=pl.ANY)
    low = jnp.bfloat16
    rows = patches.shape[0]
    return pl.pallas_call(
        encode_kernel,
        out_shape=(
            jax.ShapeDtypeStruct((KVH, rows + 16, 256), low),
            jax.ShapeDtypeStruct((text.shape[0], 256), low),
            jax.ShapeDtypeStruct(patches.shape, low),
            jax.ShapeDtypeStruct((3, rows, 640), low),
            jax.ShapeDtypeStruct((EH * rows, rows), jnp.float32),
            jax.ShapeDtypeStruct((2 * rows, 1280), low),
            jax.ShapeDtypeStruct((1280, 640), low),
        ),
        in_specs=[pl.BlockSpec(memory_space=pltpu.SMEM), vmem, vmem, vmem, vmem, any_space, any_space,
                  vmem, vmem, vmem],
        out_specs=[vmem] * 7,
        scratch_shapes=[
            pltpu.VMEM((4, 2, 8, 80, 640), low), pltpu.VMEM((4, 2, 8, 80, 512), low),
            pltpu.VMEM((2, 40, 640), low), pltpu.VMEM((2, 40, 512), low),
            pltpu.VMEM(text.shape, low), pltpu.VMEM(query_weight.shape, low), dma((2,)),
        ] + gather_scratch(),
        compiler_params=pltpu.CompilerParams(
            collective_id=0, has_side_effects=True, vmem_limit_bytes=56 * 2**20),
        name="encode",
    )(count, patches, gain, joint, kv_shard, text, query_weight, head_mask, pick, half_mask)


def reduce_peers():
    x, y, z, core = place()
    peers = [device(x, y, z, 1 - core)]
    for step in range(1, 4):
        for other in range(2):
            peers.append(device(x, lax.rem(y + step, 4), z, other))
            peers.append(device(lax.rem(x + step, 4), y, z, other))
    for step in range(1, 8):
        peers.append(device(x, y, lax.rem(z + step, 8), core))
    return peers


def reduce_steps(grads, out, from_core, chip_sum, from_near, plane_sum, from_z, from_cross, total,
                 core_send, core_recv, near_send, near_recv, z_send, z_recv, cross_send, cross_recv,
                 last_send, last_recv):
    x, y, z, core = place()
    y_hi = y // 2
    partner = device(x, y, z, 1 - core)
    spots = (y, x)
    rows, width = out.shape[1:]

    def along(axis, step):
        if axis == 0:
            return device(x, lax.rem(y + step, 4), z, core)
        return device(lax.rem(x + step, 4), y, z, core)

    def part(v, d):
        return lax.rem(spots[v] + d, 4)

    def core_copy(v, d):
        return remote(grads.at[1 - core, v, part(v, d)], from_core.at[v, d],
                      core_send.at[v, d], core_recv.at[v, d], partner)

    def near_copy(v, d):
        return remote(chip_sum.at[v, d - 1], from_near.at[v, d - 1],
                      near_send.at[v, d - 1], near_recv.at[v, d - 1], along(v, d))

    def z_copy(v, d):
        return remote(plane_sum.at[v, lax.rem(z + d, 8)], from_z.at[v, d - 1],
                      z_send.at[v, d - 1], z_recv.at[v, d - 1], device(x, y, lax.rem(z + d, 8), core))

    def cross_copy(v, d):
        slot = spots[1 - v]
        return remote(from_cross.at[v, slot], from_cross.at[v, slot],
                      cross_send.at[v, d - 1], cross_recv.at[v, d - 1], along(1 - v, d))

    def cross_arrival(v, d):
        slot = lax.rem(spots[1 - v] + 4 - d, 4)
        return remote(from_cross.at[v, slot], from_cross.at[v, slot],
                      cross_send.at[v, d - 1], cross_recv.at[v, d - 1], partner)

    def last_copy(v, i):
        peer = device(x, 2 * core + i, z, 0) if v == 0 else device(i, y, z, 1)
        slot = spots[v]
        return remote(total.at[v], out.at[slot], last_send.at[v, i], last_recv.at[slot], peer)

    def last_self(v, i):
        if v == 0:
            return jnp.logical_and(2 * core + i == y, core == 0)
        return jnp.logical_and(i == x, core == 1)

    for d in (2, 1, 3, 0):
        for v in range(2):
            core_copy(v, d).start()
    yield
    for d in (2, 1, 3):
        for v in range(2):
            core_copy(v, d).wait_recv()

            def add(k, carry, v=v, d=d):
                chip_sum[v, d - 1, k] = (
                    grads[core, v, part(v, d), k].astype(jnp.float32)
                    + from_core[v, d, k].astype(jnp.float32)
                ).astype(jnp.bfloat16)
                return carry
            lax.fori_loop(0, 8, add, 0)
            near_copy(v, d).start()
        yield
    for v in range(2):
        core_copy(v, 0).wait_recv()
        for d in range(1, 4):
            near_copy(v, d).wait_recv()

        def add(k, carry, v=v):
            sums = (grads[core, v, spots[v], k].astype(jnp.float32)
                    + from_core[v, 0, k].astype(jnp.float32))
            for d in range(3):
                sums = sums + from_near[v, d, k].astype(jnp.float32)
            plane_sum[v, k] = sums.astype(jnp.bfloat16)
            return carry
        lax.fori_loop(0, 8, add, 0)
        for d in (4, 3, 5, 2, 6, 1, 7):
            z_copy(v, d).start()
        yield
    for v in range(2):
        for d in range(1, 8):
            z_copy(v, d).wait_recv()
        sums = plane_sum[v, z].astype(jnp.float32)
        for d in range(7):
            sums = sums + from_z[v, d].astype(jnp.float32)
        from_cross[v, spots[1 - v]] = sums
        for d in (2, 1, 3):
            cross_copy(v, d).start()
    yield
    for v in range(2):
        for d in range(1, 4):
            cross_arrival(v, d).wait_recv()
        total[v] = (from_cross[v, 0] + from_cross[v, 1]) + (from_cross[v, 2] + from_cross[v, 3])
        for i in range(2 if v == 0 else 4):
            active = True if v == 0 else y_hi == core

            @pl.when(jnp.logical_and(active, jnp.logical_not(last_self(v, i))))
            def _(v=v, i=i):
                last_copy(v, i).start()

            @pl.when(jnp.logical_and(active, last_self(v, i)))
            def _(v=v):
                out[spots[v]] = total[v]
    yield
    for j in range(4):
        skip = jnp.where(core == 0, jnp.logical_and(j == y, y_hi == 0),
                         jnp.logical_and(j == x, y_hi == 1))

        @pl.when(jnp.logical_not(skip))
        def _(j=j):
            remote(out.at[j], out.at[j], last_send.at[0, 0], last_recv.at[j], partner).wait_recv()
    for v in range(2):
        for d in range(4):
            core_copy(v, d).wait_send()
        for d in range(1, 4):
            near_copy(v, d).wait_send()
            cross_copy(v, d).wait_send()
        for d in range(1, 8):
            z_copy(v, d).wait_send()
        for i in range(2 if v == 0 else 4):
            active = True if v == 0 else y_hi == core

            @pl.when(jnp.logical_and(active, jnp.logical_not(last_self(v, i))))
            def _(v=v, i=i):
                last_copy(v, i).wait_send()


def reduce_scratch():
    dma = pltpu.SemaphoreType.DMA
    block = (40, 640)
    return [
        pltpu.VMEM((2, 4, 8) + block, jnp.bfloat16),
        pltpu.VMEM((2, 3, 8) + block, jnp.bfloat16),
        pltpu.VMEM((2, 3, 8) + block, jnp.bfloat16),
        pltpu.VMEM((2, 8) + block, jnp.bfloat16),
        pltpu.VMEM((2, 7) + block, jnp.bfloat16),
        pltpu.VMEM((2, 4) + block, jnp.float32),
        pltpu.VMEM((2,) + block, jnp.float32),
        dma((2, 4)), dma((2, 4)), dma((2, 3)), dma((2, 3)), dma((2, 7)), dma((2, 7)),
        dma((2, 3)), dma((2, 3)), dma((2, 4)), dma((4,)),
    ]


def attended_steps(partial, out, from_core, chip_sum, from_y, group_sum, from_z,
                   core_send, core_recv, y_send, y_recv, z_send, z_recv):
    x, y, z, core = place()
    y_hi = y // 2
    partner = device(x, y, z, 1 - core)
    across = device(x, lax.rem(y + 2, 4), z, core)
    order = (4, 3, 5, 2, 6, 1, 7, 0)

    def spot(d):
        return lax.rem(z + d, 8)

    def core_copy(half, d):
        row = y_hi if half else 1 - y_hi
        return remote(partial.at[row, spot(d), 1 - core], from_core.at[half, d],
                      core_send.at[half, d], core_recv.at[half, d], partner)

    def y_copy(d):
        return remote(chip_sum.at[d], from_y.at[d], y_send.at[d], y_recv.at[d], across)

    def z_copy(d):
        return remote(group_sum.at[d], from_z.at[d], z_send.at[d], z_recv.at[d],
                      device(x, y, spot(d), core))

    for half in range(2):
        for d in order:
            core_copy(half, d).start()
    yield
    for d in order:
        core_copy(0, d).wait_recv()
        chip_sum[d] = (partial[1 - y_hi, spot(d), core].astype(jnp.float32)
                       + from_core[0, d].astype(jnp.float32)).astype(jnp.bfloat16)
        y_copy(d).start()
    yield
    for d in order:
        core_copy(1, d).wait_recv()
        y_copy(d).wait_recv()
        sums = (partial[y_hi, spot(d), core].astype(jnp.float32)
                + from_core[1, d].astype(jnp.float32) + from_y[d].astype(jnp.float32))
        if d:
            group_sum[d] = sums.astype(jnp.bfloat16)
            z_copy(d).start()
        else:
            out[...] = sums
    yield
    sums = out[...]
    for d in range(1, 8):
        z_copy(d).wait_recv()
        sums = sums + from_z[d].astype(jnp.float32)
    out[...] = sums
    for d in range(8):
        core_copy(0, d).wait_send()
        core_copy(1, d).wait_send()
        y_copy(d).wait_send()
        if d:
            z_copy(d).wait_send()


def attended_scratch():
    dma = pltpu.SemaphoreType.DMA
    block = (128, 256)
    return [
        pltpu.VMEM((2, 8) + block, jnp.bfloat16),
        pltpu.VMEM((8,) + block, jnp.bfloat16),
        pltpu.VMEM((8,) + block, jnp.bfloat16),
        pltpu.VMEM((8,) + block, jnp.bfloat16),
        pltpu.VMEM((8,) + block, jnp.bfloat16),
        dma((2, 8)), dma((2, 8)), dma((8,)), dma((8,)), dma((8,)), dma((8,)),
    ]


ORDER = ((4, 1), (4, 0), (3, 1), (5, 1), (3, 0), (5, 0), (2, 1), (6, 1), (2, 0), (6, 0),
         (1, 1), (7, 1), (1, 0), (7, 0), (0, 1), (0, 0))


def exchange_steps(kv, arrived, local_sem, far_send, far_recv, core_send, core_recv):
    x, y, z, core = place()
    y_hi = y // 2
    partner = device(x, y, z, 1 - core)

    def far_copy(step, turn):
        to_y = lax.rem(y + 2 * turn, 4)
        to_z = lax.rem(z + step, 8)
        head = (to_y // 2) * 4 + to_z // 2
        return remote(kv.at[head], arrived.at[y_hi, z, core], far_send.at[step, turn],
                      far_recv.at[step, turn], device(x, to_y, to_z, core))

    def source(step, turn):
        return arrived.at[lax.rem(y_hi + turn, 2), lax.rem(z + 8 - step, 8), core]

    def pass_on(step, turn):
        src = source(step, turn)
        return remote(src, src, core_send.at[step, turn], core_recv.at[step, turn], partner)

    own = pltpu.make_async_copy(kv.at[y_hi * 4 + z // 2], arrived.at[y_hi, z, core], local_sem)
    own.start()
    for step, turn in ORDER:
        if step or turn:
            far_copy(step, turn).start()
    yield
    for step, turn in reversed(ORDER):
        if step or turn:
            src = source(step, turn)
            remote(src, src, far_send.at[step, turn], far_recv.at[step, turn], partner).wait_recv()
        else:
            own.wait()
        pass_on(step, turn).start()
    yield
    for step, turn in reversed(ORDER):
        dst = arrived.at[lax.rem(y_hi + turn, 2), lax.rem(z + 8 - step, 8), 1 - core]
        remote(dst, dst, core_send.at[step, turn], core_recv.at[step, turn], partner).wait_recv()
    for step, turn in ORDER:
        pass_on(step, turn).wait_send()
        if step or turn:
            far_copy(step, turn).wait_send()


def exchange_scratch():
    dma = pltpu.SemaphoreType.DMA
    return [dma(()), dma((8, 2)), dma((8, 2)), dma((8, 2)), dma((8, 2))]


def tables():
    lane = np.arange(640)
    row = np.arange(1280)
    head_mask = (lane[None] // 80 == np.arange(8)[:, None])
    pick = (row[:, None] // 40 * 20 + row[:, None] % 20) == lane[None]
    half_mask = (row[None] % 40 // 20) == np.arange(2)[:, None]
    return tuple(jnp.asarray(a, jnp.bfloat16) for a in (head_mask, pick, half_mask))


def finish_peers():
    x, y, z, core = place()
    peers = reduce_peers()
    for step in range(8):
        if step:
            peers.append(device(x, lax.rem(y + 2, 4), lax.rem(z + step, 8), core))
    return peers


def finish_kernel(count_ref, length_ref, kv, queries, normed, qkv, probs_ref, spread, out_weight,
                  cotangent, mask_ids, head_mask, pick, half_mask, output_weight,
                  sums_out, attended_out,
                  arrived, scores, grads, partial, head_rows, grad_rows, weight_in, load_sem, *rest):
    split = len(exchange_scratch())
    middle = split + len(reduce_scratch())
    meet(finish_peers())
    exchange = exchange_steps(kv, arrived, *rest[:split])
    reduce = reduce_steps(grads, sums_out, *rest[split:middle])
    attend = attended_steps(partial, attended_out, *rest[middle:])
    next(exchange)
    load = pltpu.make_async_copy(output_weight, weight_in, load_sem)
    load.start()

    rows = cotangent.shape[0]
    masks = head_mask[...]
    low = jnp.bfloat16
    live_row = lax.broadcasted_iota(jnp.int32, (rows, 1), 0) < count_ref[0] * PATCH
    upstream = jnp.where(live_row, cotangent[...].astype(jnp.float32), 0.0).astype(low)
    sides = jnp.concatenate([upstream[:, :640], upstream[:, 640:]], axis=0)
    backs = dot(sides, out_weight[...], ((1,), (1,)))
    backs = (backs[:rows] * half_mask[0:1].astype(jnp.float32)
             + backs[rows:] * half_mask[1:2].astype(jnp.float32))
    high = backs.astype(low)
    rest_low = (backs - high.astype(jnp.float32)).astype(low)
    picked = dot(jnp.concatenate([high, rest_low], axis=0), pick[...])
    grad_context = (picked[:rows] + picked[rows:]).astype(low)
    grad_rows[...] = head_stack(grad_context, masks)
    head_rows[...] = head_stack(qkv[0], masks)
    probs = probs_ref[...]
    grad_probs = dot(grad_rows[...], qkv[2], ((1,), (1,)))
    inner = jnp.sum(probs * grad_probs, axis=-1, keepdims=True)
    grad_scores = (probs * (grad_probs - inner) * EHD ** (-0.5)).astype(low)
    grad_values = dot(probs.astype(low).T, grad_rows[...]).astype(low)
    grad_keys = dot(grad_scores.T, head_rows[...]).astype(low)
    grad_queries = head_pick(dot(grad_scores, qkv[1]), masks).astype(low)

    def store(j, left, right):
        for y_hi in range(2):
            block = dot(left[640 * y_hi:640 * (y_hi + 1)], right).astype(low).astype(jnp.float32)
            for z in range(8):
                for core in range(2):
                    start = 80 * z + 40 * core
                    grads[y_hi, core, j, z] = block[start:start + 40].astype(low)

    turned = normed[...].T
    for j, right in enumerate((grad_queries, grad_keys, grad_values)):
        store(j, turned, right)
    store(3, spread[...].T, sides)
    next(reduce)
    next(reduce)
    next(reduce)
    next(reduce)

    next(exchange)
    for _ in exchange:
        pass
    next(reduce)
    next(reduce)
    text = queries.shape[0]
    stacked = jnp.concatenate([queries[:, :HD], queries[:, HD:]], axis=0)
    images = jnp.concatenate([mask_ids[...], mask_ids[...]], axis=0)
    tile_of = lax.broadcasted_iota(jnp.int32, (1, rows), 1)
    top = jnp.full((2 * text, 1), NEG, jnp.float32)
    seen = jnp.zeros((2 * text, 1), jnp.float32)
    for i in range(32):
        where = (i // 16, i // 2 % 8, i % 2)
        counts = arrived[where + (pl.ds(rows, 16), pl.ds(0, 128))][0:1].astype(jnp.float32)
        live = tile_of.astype(jnp.float32) < counts * float(PATCH)
        allowed = jnp.logical_and(live, i < images)
        keys = arrived[where + (pl.ds(0, rows), pl.ds(0, HD))]
        piece = dot(stacked, keys, ((1,), (1,))) * HD ** (-0.5)
        piece = jnp.where(allowed, piece, NEG)
        scores[:, i * 128:(i + 1) * 128] = piece
        top = jnp.maximum(top, jnp.max(piece, axis=-1, keepdims=True))
        seen = jnp.maximum(seen, jnp.max(jnp.where(allowed, 1.0, 0.0), axis=-1, keepdims=True))
    total = jnp.zeros((2 * text, 1), jnp.float32)
    for i in range(32):
        piece = jnp.exp(scores[:, i * 128:(i + 1) * 128] - top)
        scores[:, i * 128:(i + 1) * 128] = piece
        total = total + jnp.sum(piece, axis=-1, keepdims=True)
    context = jnp.zeros((2 * text, HD), jnp.float32)
    for i in range(32):
        where = (i // 16, i // 2 % 8, i % 2)
        low_probs = (scores[:, i * 128:(i + 1) * 128] / total).astype(low)
        context = context + dot(low_probs, arrived[where + (pl.ds(0, rows), pl.ds(HD, HD))])
    context = context.astype(low)
    context = jnp.concatenate([context[:text], context[text:]], axis=1)
    load.wait()

    def project(block, carry):
        columns = pl.ds(pl.multiple_of(block * 256, 256), 256)
        partial[block // 16, lax.rem(block // 2, 8), lax.rem(block, 2)] = dot(
            context, weight_in[:, columns]).astype(low)
        return carry
    lax.fori_loop(0, 32, project, 0)
    next(attend)
    next(reduce)
    next(attend)
    next(attend)
    for _ in reduce:
        pass
    for _ in attend:
        pass
    rows_live = jnp.logical_and(
        seen[:text] > 0.0,
        lax.broadcasted_iota(jnp.int32, (text, 1), 0) < length_ref[0])
    attended_out[...] = jnp.where(rows_live, attended_out[...], 0.0)


def finish(count, length, kv, queries, normed, qkv, probs, spread, out_weight, cotangent, mask_ids,
           head_mask, pick, half_mask, output_weight):
    dma = pltpu.SemaphoreType.DMA
    vmem = pl.BlockSpec(memory_space=pltpu.VMEM)
    smem = pl.BlockSpec(memory_space=pltpu.SMEM)
    low = jnp.bfloat16
    rows = cotangent.shape[0]
    text = queries.shape[0]
    return pl.pallas_call(
        finish_kernel,
        out_shape=(jax.ShapeDtypeStruct((4, 40, 640), jnp.float32),
                   jax.ShapeDtypeStruct((text, 256), jnp.float32)),
        in_specs=[smem, smem] + [vmem] * 12 + [pl.BlockSpec(memory_space=pl.ANY)],
        out_specs=[vmem] * 2,
        scratch_shapes=[
            pltpu.VMEM((2, 8, 2, rows + 16, 256), low), pltpu.VMEM((2 * text, 32 * 128), jnp.float32),
            pltpu.VMEM((2, 2, 4, 8, 40, 640), low), pltpu.VMEM((2, 8, 2, text, 256), low),
            pltpu.VMEM((EH * rows, 640), low), pltpu.VMEM((EH * rows, 640), low),
            pltpu.VMEM(output_weight.shape, low), dma(()),
        ] + exchange_scratch() + reduce_scratch() + attended_scratch(),
        compiler_params=pltpu.CompilerParams(
            collective_id=1, has_side_effects=True, vmem_limit_bytes=60 * 2**20),
        name="finish",
    )(count, length, kv, queries, normed, qkv, probs, spread, out_weight, cotangent, mask_ids,
      head_mask, pick, half_mask, output_weight)


def per_device(
    patches,
    cotangent,
    tile_counts,
    ln_gain,
    qkv_weight,
    out_weight,
    text_states,
    mask_ids,
    text_lengths,
    gate_value,
    query_weight,
    kv_weight,
    output_weight,
):
    fsdp_index = lax.axis_index("fsdp")
    head_mask, pick, half_mask = tables()
    out_halves = jnp.transpose(out_weight.reshape(-1, 2, 640), (1, 0, 2)).reshape(-1, 640)
    joint = jnp.concatenate([qkv_weight, out_halves], axis=1)
    kv, queries, normed, qkv, probs, spread, out_rows = encode(
        tile_counts, patches, ln_gain[None], joint, kv_weight, text_states, query_weight,
        head_mask, pick, half_mask)
    sums, attended = finish(
        tile_counts, text_lengths, kv, queries, normed, qkv, probs, spread, out_rows, cotangent,
        mask_ids[:, None], head_mask, pick, half_mask, output_weight)
    sum_qkv = jnp.transpose(sums[:3], (1, 0, 2)).reshape(40, 1920)
    sum_out = jnp.transpose(sums[3].reshape(2, 20, 640), (1, 0, 2)).reshape(20, 1280)
    col_width = attended.shape[1]
    text_cols = lax.dynamic_slice_in_dim(text_states, fsdp_index * col_width, col_width, 1)
    result = text_cols.astype(jnp.float32) + jnp.tanh(gate_value[0]) * attended
    return (sum_qkv, sum_out, result.astype(jnp.bfloat16))


def solution(mesh):
    placed = (
        P(("dp", "fsdp"), None),
        P(("dp", "fsdp"), None),
        P(("dp", "fsdp")),
        P(),
        P("fsdp", None),
        P("fsdp", None),
        P("dp", None),
        P("dp"),
        P("dp"),
        P(),
        P(None, "fsdp"),
        P("fsdp", None),
        P("fsdp", None),
    )
    return jax.shard_map(
        per_device,
        mesh=mesh,
        in_specs=placed,
        out_specs=(P("fsdp", None), P("fsdp", None), P("dp", "fsdp")),
        check_vma=False,
    )
```

time: 270 us -> 172 us (0.64)
  local copies, waits for them, and re-layouts: 53.2 us -> 6.31 us
  matrix products: 27.7 us -> 0 us
  Pallas kernels: 174 us -> 160 us
  other arithmetic: 9.93 us -> 3.17 us
    reshape x9 -> x0, local copies, waits for them, and re-layouts: 24.6 us -> none  [the longest x2 17.2 us: per_device(): parts = grad_qkv.astype(jnp.bfloat16).reshape(2, 8, 2, 40, 3, 640)]
    dot_general x19 -> x0, matrix products: 24.3 us -> none  [the longest x1 4.23 us: per_device(): jnp.dot(context, output_weight, preferred_element_type=jnp.float32)]
    pallas_call x4 -> x2, Pallas kernels: 174 us -> 160 us  [the longest x1 89.4 us: finish(): pl.pallas_call(finish_kernel, out_shape=(jax.ShapeDtypeStruct((4, 40, 640...]
    slice x4 -> x0, local copies, waits for them, and re-layouts: 12.4 us -> none  [the longest x1 5.38 us: per_device(): full_out = joint_full[3].reshape(32, 2, 20, 640)]
    convert_element_type x5 -> x0, local copies, waits for them, and re-layouts: 4.76 us -> none  [the longest x1 4.1 us: per_device(): partial_out.astype(jnp.bfloat16).reshape(text_count, 2, 8, 2, 256)]
    concatenate x2 -> x0, other arithmetic: 3.46 us -> none  [the longest x1 3.41 us: per_device(): sums = reduce_grads(jnp.concatenate([parts, halves], axis=2))]
    sub x2 -> x0, matrix products: 3.45 us -> none  [the longest x1 3.07 us: per_device(): weights = jnp.exp(scores - row_top)]
where the time goes in v3:
time: 172 us
  Pallas kernels  160 us (93%)
  local copies, waits for them, and re-layouts  6.31 us (4%)
  other arithmetic  3.17 us (2%)
  between operations  2.68 us (2%)
    pallas_call x1, Pallas kernels, finish(): pl.pallas_call(finish_kernel, out_shape=(jax.ShapeDtypeStruct((4, 40, 640...  89.4 us
    pallas_call x1, Pallas kernels, encode(): pl.pallas_call(encode_kernel, out_shape=(jax.ShapeDtypeStruct((KVH, rows...  70.2 us

profile of v3, /device:TPU:1, one launch (start us, length us, event | category | flops | bytes accessed | tf_op | source)
XLA Modules:
  0.0 171.7 jit_solution(7247751133176174660)
XLA Ops:
  1.3 0.9 reshape.19
  2.2 1.6 pad_maximum_fusion.joint
  3.8 1.3 broadcast_in_dim.6.gain
  5.1 0.0 copy-start
  5.1 70.2 %encode.1 = (bf16[8,144,256]{2,1,0:T(8,128)(2,1)}, bf16[128,256]{1,0:T(8,128)(2,1)}, bf16[128,1280]{1,0:T(8,128)(2,1)}, bf16[3,128,640]{2,1,0:T(8,128)(2,1)}, f3...) custom-call(s32[1]{0:T(128)S(6)} %copy.33.count_ref, bf16[128,1280]{1,0:T(8,128)(2,1)} %patches.1, ...), custom_call_target="tpu_custom_call" | custom-call | tf_op jit(solution)/shard_map/encode/pallas_call | solution.py:295
  75.3 0.0 copy-done
  75.3 0.7 copy.26.mask_ids
  76.7 89.4 %finish.1 = (f32[4,40,640]{2,1,0:T(8,128)}, f32[128,256]{1,0:T(8,128)}) custom-call(s32[1]{0:T(128)S(6)} %copy.33.count_ref, s32[1]{0:T(128)S(6)} %copy.34.length_ref, bf16[8,144,256]{2,1,0:T(8,128)(2,1)} %get-tuple-element.12.kv, bf16[128,256]{1,0:T(8,128)(2,1)} %get-tuple-element.13.queries, bf16[128,1280]{1,0:T(8,128)(2,1)} %get-tuple-element.14.normed, ...), custom_call_target="tpu_custom_call" | custom-call | tf_op jit(solution)/shard_map/finish/pallas_call | solution.py:735
  166.7 1.6 add_convert_fusion
  168.3 1.0 slice_bitcast_fusion
  169.3 0.7 copy.29
  170.0 0.9 slice.7
  170.9 0.1 copy.28
  171.1 0.7 copy.30
  (4 shorter events, 0.1 us)
Async XLA Ops:
  5.1 70.2 %copy-start = (s32[128]{0:T(128)S(1)}, s32[128]{0:T(128)}, u32[]{:S(2)}) copy-start(s32[128]{0:T(128)} %param.23) | copy-start | bytes 1540

commit v4 on v3

--- a/solution.py
+++ b/solution.py
@@ -11,7 +11,9 @@
 PATCH = 32
 HD = 128
 KVH = 8
-LAG = 3
+LAG = 0
+NEAR_LAG = 3
+FAR_LAG = 3
 
 EPS = 1e-05
 NEG = -1e30
@@ -62,6 +64,7 @@
         peers.append(device(lax.rem(x + step, 4), y, z, core))
     for step in (1, 7):
         peers.append(device(x, y, lax.rem(z + step, 8), core))
+    peers.append(device(x, y, z + 1 - 2 * lax.rem(z, 2), 1 - core))
     return peers
 
 
@@ -81,6 +84,8 @@
         return my_y + turned(where) * (x - my_y)
 
     def columns(spot):
+        if t == 0:
+            return shard.at[spot]
         return shard.at[:, pl.ds(pl.multiple_of(spot * width, 128), width)]
 
     def unit_z(u):
@@ -154,7 +159,7 @@
     def _():
         to_partner().start()
     yield
-    for u in range(10):
+    for u in range(8 + NEAR_LAG + FAR_LAG):
         if u == 0:
             @pl.when(mine)
             def _():
@@ -176,13 +181,13 @@
         if u < 8:
             near_copy(0, u).start()
             near_copy(1, u).start()
-        if 1 <= u < 9:
+        if 0 <= u - NEAR_LAG < 8:
             for side in range(2):
-                near_arrival(side, u - 1).wait_recv()
-            far_copy(u - 1).start()
-        if 2 <= u:
-            far_arrival(u - 2).wait_recv()
-            pass_on(u - 2).start()
+                near_arrival(side, u - NEAR_LAG).wait_recv()
+            far_copy(u - NEAR_LAG).start()
+        if 0 <= u - NEAR_LAG - FAR_LAG:
+            far_arrival(u - NEAR_LAG - FAR_LAG).wait_recv()
+            pass_on(u - NEAR_LAG - FAR_LAG).start()
         yield
     to_mirror().wait_send()
 
@@ -216,51 +221,68 @@
     return total
 
 
-def encode_kernel(count_ref, patches, gain, joint, kv_shard, text, query_weight, head_mask, pick,
-                  half_mask, kv_out, queries_out, normed_out, qkv_out, probs_out, spread_out, out_weight,
-                  joint_full, kv_full, joint_pair, kv_pair, text_in, query_in, local_sem, *sems):
+def query_copy(queries, send_sem, recv_sem, offset):
+    x, y, z, core = place()
+    side = lax.rem(z, 2)
+    peer = device(x, y, z + (offset // 2) * (1 - 2 * side), lax.rem(core + offset, 2))
+    slot = queries.at[2 * side + core]
+    return remote(slot, slot, send_sem.at[offset - 1], recv_sem.at[offset - 1], peer)
+
+
+def encode_kernel(count_ref, patches, gain, qkv_shard, out_shard, kv_shard, text, query_weight, head_mask,
+                  pick, half_mask, kv_out, queries_out, normed_out, qkv_out, probs_out, spread_out,
+                  out_weight, joint, joint_full, kv_full, joint_pair, kv_pair, text_in, query_in,
+                  local_sem, query_send, query_recv, *sems):
+    for part in range(3):
+        joint[part] = qkv_shard[:, part * 640:(part + 1) * 640]
+    shard = out_shard[...].astype(jnp.float32)
+    joint[3] = jnp.concatenate([shard[:, :640], shard[:, 640:]], axis=0).astype(jnp.bfloat16)
     meet(gather_peers())
     first = gather_steps(0, joint, joint_full, joint_pair, *sems)
     second = gather_steps(1, kv_shard, kv_full, kv_pair, *sems)
-    next(first)
-    next(second)
+    next(first, None)
+    next(second, None)
     load_text = pltpu.make_async_copy(text, text_in, local_sem.at[0])
     load_query = pltpu.make_async_copy(query_weight, query_in, local_sem.at[1])
     load_text.start()
     load_query.start()
 
-    next(first)
+    next(first, None)
     inputs = patches[...].astype(jnp.float32)
     centred = inputs - jnp.mean(inputs, axis=-1, keepdims=True)
     spread = jnp.mean(centred * centred, axis=-1, keepdims=True)
-    normed = (centred * lax.rsqrt(spread + EPS) * gain[...]).astype(jnp.bfloat16)
+    normed = (centred * lax.rsqrt(spread + EPS) * gain[...].reshape(1, -1)).astype(jnp.bfloat16)
     normed_out[...] = normed
-    next(first)
+    next(first, None)
     load_text.wait()
     load_query.wait()
-    queries = jnp.zeros(queries_out.shape, jnp.float32)
-    for step in range(8):
-        queries = queries + dot(text_in[:, step * 1024:(step + 1) * 1024],
-                                query_in[step * 1024:(step + 1) * 1024, :])
-        next(first)
+    queries = jnp.zeros(queries_out.shape[1:], jnp.float32)
+    for step in range(6 + NEAR_LAG + FAR_LAG):
+        if step < 8:
+            queries = queries + dot(text_in[:, step * 1024:(step + 1) * 1024],
+                                    query_in[step * 1024:(step + 1) * 1024, :])
+        next(first, None)
         if step >= LAG:
-            next(second)
-    queries_out[...] = queries.astype(jnp.bfloat16)
-    next(first)
+            next(second, None)
+    _, _, z, core = place()
+    queries_out[2 * lax.rem(z, 2) + core] = queries.astype(jnp.bfloat16)
+    for offset in range(1, 4):
+        query_copy(queries_out, query_send, query_recv, offset).start()
+    next(first, None)
 
     masks = head_mask[...]
     rows = inputs.shape[0]
-    next(second)
+    next(second, None)
     query = dot(normed_out[...], joint_full[0].reshape(1280, 640)).astype(jnp.bfloat16)
     qkv_out[0] = query
-    next(second)
+    next(second, None)
     key = dot(normed_out[...], joint_full[1].reshape(1280, 640)).astype(jnp.bfloat16)
     qkv_out[1] = key
-    next(second)
+    next(second, None)
     value = dot(normed_out[...], joint_full[2].reshape(1280, 640)).astype(jnp.bfloat16)
     qkv_out[2] = value
     out_weight[...] = joint_full[3].reshape(1280, 640)
-    next(second)
+    next(second, None)
     live_key = lax.broadcasted_iota(jnp.int32, (1, rows), 1) < count_ref[0] * PATCH
     live_row = lax.broadcasted_iota(jnp.int32, (rows, 1), 0) < count_ref[0] * PATCH
     scores = dot(head_stack(query, masks), key, ((1,), (1,))) * EHD ** (-0.5)
@@ -268,7 +290,7 @@
     weights = jnp.exp(scores - jnp.max(scores, axis=-1, keepdims=True))
     probs = weights / jnp.sum(weights, axis=-1, keepdims=True)
     probs_out[...] = probs
-    next(second)
+    next(second, None)
     context = head_pick(dot(probs.astype(jnp.bfloat16), value), masks).astype(jnp.bfloat16)
     both = dot(context, pick[...], ((1,), (1,))).astype(jnp.bfloat16)
     halves = jnp.concatenate([both * half_mask[0:1], both * half_mask[1:2]], axis=0)
@@ -282,11 +304,13 @@
         piece = dot(vision, kv_full[part].reshape(1280, 512)).astype(jnp.bfloat16)
         for side in range(2):
             kv_out[2 * part + side, pl.ds(0, rows), :] = piece[:, side * 256:(side + 1) * 256]
+    for offset in range(1, 4):
+        query_copy(queries_out, query_send, query_recv, offset).wait()
     number = jnp.full((KVH, 16, 256), count_ref[0].astype(jnp.float32)).astype(jnp.bfloat16)
     kv_out[:, pl.ds(rows, 16), :] = number
 
 
-def encode(count, patches, gain, joint, kv_shard, text, query_weight, head_mask, pick, half_mask):
+def encode(count, patches, gain, qkv_shard, out_shard, kv_shard, text, query_weight, head_mask, pick, half_mask):
     dma = pltpu.SemaphoreType.DMA
     vmem = pl.BlockSpec(memory_space=pltpu.VMEM)
     any_space = pl.BlockSpec(memory_space=pl.ANY)
@@ -296,25 +320,25 @@
         encode_kernel,
         out_shape=(
             jax.ShapeDtypeStruct((KVH, rows + 16, 256), low),
-            jax.ShapeDtypeStruct((text.shape[0], 256), low),
+            jax.ShapeDtypeStruct((4, text.shape[0], 256), low),
             jax.ShapeDtypeStruct(patches.shape, low),
             jax.ShapeDtypeStruct((3, rows, 640), low),
             jax.ShapeDtypeStruct((EH * rows, rows), jnp.float32),
             jax.ShapeDtypeStruct((2 * rows, 1280), low),
             jax.ShapeDtypeStruct((1280, 640), low),
         ),
-        in_specs=[pl.BlockSpec(memory_space=pltpu.SMEM), vmem, vmem, vmem, vmem, any_space, any_space,
-                  vmem, vmem, vmem],
+        in_specs=[pl.BlockSpec(memory_space=pltpu.SMEM)] + [vmem] * 5 + [any_space] * 2 + [vmem] * 3,
         out_specs=[vmem] * 7,
         scratch_shapes=[
-            pltpu.VMEM((4, 2, 8, 80, 640), low), pltpu.VMEM((4, 2, 8, 80, 512), low),
+            pltpu.VMEM((4, 40, 640), low), pltpu.VMEM((4, 2, 8, 80, 640), low), pltpu.VMEM((4, 2, 8, 80, 512), low),
             pltpu.VMEM((2, 40, 640), low), pltpu.VMEM((2, 40, 512), low),
             pltpu.VMEM(text.shape, low), pltpu.VMEM(query_weight.shape, low), dma((2,)),
+            dma((3,)), dma((3,)),
         ] + gather_scratch(),
         compiler_params=pltpu.CompilerParams(
             collective_id=0, has_side_effects=True, vmem_limit_bytes=56 * 2**20),
         name="encode",
-    )(count, patches, gain, joint, kv_shard, text, query_weight, head_mask, pick, half_mask)
+    )(count, patches, gain, qkv_shard, out_shard, kv_shard, text, query_weight, head_mask, pick, half_mask)
 
 
 def reduce_peers():
@@ -545,55 +569,45 @@
     ]
 
 
-ORDER = ((4, 1), (4, 0), (3, 1), (5, 1), (3, 0), (5, 0), (2, 1), (6, 1), (2, 0), (6, 0),
-         (1, 1), (7, 1), (1, 0), (7, 0), (0, 1), (0, 0))
-
-
-def exchange_steps(kv, arrived, local_sem, far_send, far_recv, core_send, core_recv):
-    x, y, z, core = place()
-    y_hi = y // 2
-    partner = device(x, y, z, 1 - core)
+NEAREST = ((0, 0), (1, 0), (0, 1), (1, 1), (2, 0), (2, 1), (3, 0), (3, 1))
+
+
+def image_at(step, turn):
+    x, y, z, core = place()
+    from_z = lax.rem(z + (2 * lax.rem(z, 2) - 1) * step + 8, 8)
+    return lax.rem(y // 2 + turn, 2) * 16 + from_z * 2 + core
+
+
+def exchange_steps(kv, arrived, local_sem, far_send, far_recv):
+    x, y, z, core = place()
 
     def far_copy(step, turn):
         to_y = lax.rem(y + 2 * turn, 4)
-        to_z = lax.rem(z + step, 8)
+        to_z = lax.rem(z + step * (1 - 2 * lax.rem(z + step, 2)) + 8, 8)
         head = (to_y // 2) * 4 + to_z // 2
-        return remote(kv.at[head], arrived.at[y_hi, z, core], far_send.at[step, turn],
-                      far_recv.at[step, turn], device(x, to_y, to_z, core))
-
-    def source(step, turn):
-        return arrived.at[lax.rem(y_hi + turn, 2), lax.rem(z + 8 - step, 8), core]
-
-    def pass_on(step, turn):
-        src = source(step, turn)
-        return remote(src, src, core_send.at[step, turn], core_recv.at[step, turn], partner)
-
-    own = pltpu.make_async_copy(kv.at[y_hi * 4 + z // 2], arrived.at[y_hi, z, core], local_sem)
+        return remote(kv.at[head], arrived.at[turn, step], far_send.at[turn, step],
+                      far_recv.at[turn, step], device(x, to_y, to_z, core))
+
+    own = pltpu.make_async_copy(kv.at[(y // 2) * 4 + z // 2], arrived.at[0, 0], local_sem)
     own.start()
-    for step, turn in ORDER:
+    for step, turn in reversed(NEAREST):
         if step or turn:
             far_copy(step, turn).start()
     yield
-    for step, turn in reversed(ORDER):
+    for step, turn in NEAREST:
         if step or turn:
-            src = source(step, turn)
-            remote(src, src, far_send.at[step, turn], far_recv.at[step, turn], partner).wait_recv()
+            far_copy(step, turn).wait_recv()
         else:
             own.wait()
-        pass_on(step, turn).start()
-    yield
-    for step, turn in reversed(ORDER):
-        dst = arrived.at[lax.rem(y_hi + turn, 2), lax.rem(z + 8 - step, 8), 1 - core]
-        remote(dst, dst, core_send.at[step, turn], core_recv.at[step, turn], partner).wait_recv()
-    for step, turn in ORDER:
-        pass_on(step, turn).wait_send()
+        yield
+    for step, turn in NEAREST:
         if step or turn:
             far_copy(step, turn).wait_send()
 
 
 def exchange_scratch():
     dma = pltpu.SemaphoreType.DMA
-    return [dma(()), dma((8, 2)), dma((8, 2)), dma((8, 2)), dma((8, 2))]
+    return [dma(()), dma((2, 4)), dma((2, 4))]
 
 
 def tables():
@@ -611,22 +625,28 @@
     for step in range(8):
         if step:
             peers.append(device(x, lax.rem(y + 2, 4), lax.rem(z + step, 8), core))
+    peers.append(device(x, y, z + 1 - 2 * lax.rem(z, 2), 1 - core))
     return peers
 
 
-def finish_kernel(count_ref, length_ref, kv, queries, normed, qkv, probs_ref, spread, out_weight,
-                  cotangent, mask_ids, head_mask, pick, half_mask, output_weight,
-                  sums_out, attended_out,
-                  arrived, scores, grads, partial, head_rows, grad_rows, weight_in, load_sem, *rest):
+def finish_kernel(count_ref, length_ref, gate_ref, kv, queries, normed, qkv, probs_ref, spread, out_weight,
+                  cotangent, mask_ids, head_mask, pick, half_mask, output_weight, text_states,
+                  qkv_out, out_out, result_out,
+                  arrived, scores, grads, partial, head_rows, grad_rows, weight_in, sums, attended, text_in,
+                  part_out, part_in, stat_out, stat_in, part_send, part_recv, stat_send, stat_recv,
+                  load_sem, *rest):
     split = len(exchange_scratch())
     middle = split + len(reduce_scratch())
     meet(finish_peers())
     exchange = exchange_steps(kv, arrived, *rest[:split])
-    reduce = reduce_steps(grads, sums_out, *rest[split:middle])
-    attend = attended_steps(partial, attended_out, *rest[middle:])
+    reduce = reduce_steps(grads, sums, *rest[split:middle])
+    attend = attended_steps(partial, attended, *rest[middle:])
     next(exchange)
-    load = pltpu.make_async_copy(output_weight, weight_in, load_sem)
+    load = pltpu.make_async_copy(output_weight, weight_in, load_sem.at[0])
     load.start()
+    columns = pl.ds(pl.multiple_of(lax.axis_index("fsdp") * 256, 256), 256)
+    load_text = pltpu.make_async_copy(text_states.at[:, columns], text_in, load_sem.at[1])
+    load_text.start()
 
     rows = cotangent.shape[0]
     masks = head_mask[...]
@@ -668,40 +688,83 @@
     next(reduce)
     next(reduce)
 
-    next(exchange)
+    text = queries.shape[1]
+    stacked = jnp.concatenate(
+        [queries[g, :, side * HD:(side + 1) * HD] for g in range(4) for side in range(2)], axis=0)
+    square = (text, text)
+    diagonal = (lax.broadcasted_iota(jnp.int32, square, 0) == lax.broadcasted_iota(jnp.int32, square, 1))
+    images = jnp.sum(jnp.where(diagonal, mask_ids[...].astype(jnp.float32).reshape(1, text), 0.0),
+                     axis=1, keepdims=True)
+    images = jnp.concatenate([images] * 8, axis=0)
+    tile_of = lax.broadcasted_iota(jnp.int32, (1, rows), 1).astype(jnp.float32)
+    top = jnp.full((8 * text, 1), NEG, jnp.float32)
+    for i, (step, turn) in enumerate(NEAREST):
+        next(exchange)
+        counts = arrived[turn, step, pl.ds(rows, 16), pl.ds(0, 128)][0:1].astype(jnp.float32)
+        number = image_at(step, turn).astype(jnp.float32)
+        allowed = jnp.logical_and(tile_of < counts * float(PATCH), number < images)
+        piece = dot(stacked, arrived[turn, step, pl.ds(0, rows), pl.ds(0, HD)], ((1,), (1,)))
+        piece = jnp.where(allowed, piece * HD ** (-0.5), NEG)
+        scores[:, i * 128:(i + 1) * 128] = piece
+        top = jnp.maximum(top, jnp.max(piece, axis=-1, keepdims=True))
+    total = jnp.zeros((8 * text, 1), jnp.float32)
+    context = jnp.zeros((8 * text, HD), jnp.float32)
+    for i, (step, turn) in enumerate(NEAREST):
+        piece = jnp.exp(scores[:, i * 128:(i + 1) * 128] - top)
+        total = total + jnp.sum(piece, axis=-1, keepdims=True)
+        context = context + dot(piece.astype(low), arrived[turn, step, pl.ds(0, rows), pl.ds(HD, HD)])
+    context = context / total
+    total = jnp.where(top > 0.5 * NEG, total, 0.0)
     for _ in exchange:
         pass
-    next(reduce)
-    next(reduce)
-    text = queries.shape[0]
-    stacked = jnp.concatenate([queries[:, :HD], queries[:, HD:]], axis=0)
-    images = jnp.concatenate([mask_ids[...], mask_ids[...]], axis=0)
-    tile_of = lax.broadcasted_iota(jnp.int32, (1, rows), 1)
-    top = jnp.full((2 * text, 1), NEG, jnp.float32)
+    scores[:, 0:128] = context
+    lane = lax.broadcasted_iota(jnp.int32, (1, 128), 1)
+    scores[:, 128:256] = jnp.where(lane < 4, top, total)
+    x, y, z, core = place()
+    side = lax.rem(z, 2)
+
+    def own_rows(group):
+        return pl.ds(pl.multiple_of(group * 2 * text, 256), 2 * text)
+
+    def context_copy(offset):
+        peer = device(x, y, z + (offset // 2) * (1 - 2 * side), lax.rem(core + offset, 2))
+        return remote(part_out.at[offset - 1], part_in.at[offset - 1], part_send.at[offset - 1],
+                      part_recv.at[offset - 1], peer)
+
+    def stat_copy(offset):
+        peer = device(x, y, z + (offset // 2) * (1 - 2 * side), lax.rem(core + offset, 2))
+        return remote(stat_out.at[offset - 1], stat_in.at[offset - 1], stat_send.at[offset - 1],
+                      stat_recv.at[offset - 1], peer)
+
+    for offset in (2, 3, 1):
+        group = 2 * lax.rem(side + offset // 2, 2) + lax.rem(core + offset, 2)
+        part_out[offset - 1] = scores[own_rows(group), 0:128].astype(low)
+        context_copy(offset).start()
+        stat_out[offset - 1] = scores[own_rows(group), 128:256].T[0:8]
+        stat_copy(offset).start()
+    group = 2 * side + core
+    parts = [scores[own_rows(group), 0:128]]
+    tops = [scores[own_rows(group), 128:129]]
+    totals = [scores[own_rows(group), 132:133]]
+    for offset in range(1, 4):
+        context_copy(offset).wait_recv()
+        stat_copy(offset).wait_recv()
+        stats = jnp.concatenate([stat_in[offset - 1]] * 16, axis=0).T
+        parts.append(part_in[offset - 1].astype(jnp.float32))
+        tops.append(stats[:, 0:1])
+        totals.append(stats[:, 4:5])
+    top = jnp.maximum(jnp.maximum(tops[0], tops[1]), jnp.maximum(tops[2], tops[3]))
     seen = jnp.zeros((2 * text, 1), jnp.float32)
-    for i in range(32):
-        where = (i // 16, i // 2 % 8, i % 2)
-        counts = arrived[where + (pl.ds(rows, 16), pl.ds(0, 128))][0:1].astype(jnp.float32)
-        live = tile_of.astype(jnp.float32) < counts * float(PATCH)
-        allowed = jnp.logical_and(live, i < images)
-        keys = arrived[where + (pl.ds(0, rows), pl.ds(0, HD))]
-        piece = dot(stacked, keys, ((1,), (1,))) * HD ** (-0.5)
-        piece = jnp.where(allowed, piece, NEG)
-        scores[:, i * 128:(i + 1) * 128] = piece
-        top = jnp.maximum(top, jnp.max(piece, axis=-1, keepdims=True))
-        seen = jnp.maximum(seen, jnp.max(jnp.where(allowed, 1.0, 0.0), axis=-1, keepdims=True))
-    total = jnp.zeros((2 * text, 1), jnp.float32)
-    for i in range(32):
-        piece = jnp.exp(scores[:, i * 128:(i + 1) * 128] - top)
-        scores[:, i * 128:(i + 1) * 128] = piece
-        total = total + jnp.sum(piece, axis=-1, keepdims=True)
     context = jnp.zeros((2 * text, HD), jnp.float32)
-    for i in range(32):
-        where = (i // 16, i // 2 % 8, i % 2)
-        low_probs = (scores[:, i * 128:(i + 1) * 128] / total).astype(low)
-        context = context + dot(low_probs, arrived[where + (pl.ds(0, rows), pl.ds(HD, HD))])
-    context = context.astype(low)
+    for k in range(4):
+        share = totals[k] * jnp.exp(tops[k] - top)
+        seen = seen + share
+        context = context + share * parts[k]
+    context = (context / jnp.where(seen > 0.0, seen, 1.0)).astype(low)
     context = jnp.concatenate([context[:text], context[text:]], axis=1)
+    for offset in range(1, 4):
+        context_copy(offset).wait_send()
+        stat_copy(offset).wait_send()
     load.wait()
 
     def project(block, carry):
@@ -712,7 +775,9 @@
     lax.fori_loop(0, 32, project, 0)
     next(attend)
     next(reduce)
+    next(reduce)
     next(attend)
+    next(reduce)
     next(attend)
     for _ in reduce:
         pass
@@ -721,34 +786,47 @@
     rows_live = jnp.logical_and(
         seen[:text] > 0.0,
         lax.broadcasted_iota(jnp.int32, (text, 1), 0) < length_ref[0])
-    attended_out[...] = jnp.where(rows_live, attended_out[...], 0.0)
-
-
-def finish(count, length, kv, queries, normed, qkv, probs, spread, out_weight, cotangent, mask_ids,
-           head_mask, pick, half_mask, output_weight):
+    gate = jnp.tanh(jnp.full((1, 256), gate_ref[0], jnp.float32))
+    load_text.wait()
+    result_out[...] = (text_in[...].astype(jnp.float32)
+                       + gate * jnp.where(rows_live, attended[...], 0.0)).astype(low)
+    for j in range(3):
+        qkv_out[:, j * 640:(j + 1) * 640] = sums[j]
+    last = sums[3]
+    out_out[:, 0:640] = last[0:20]
+    out_out[:, 640:1280] = last[20:40]
+
+
+def finish(count, length, gate, kv, queries, normed, qkv, probs, spread, out_weight, cotangent, mask_ids,
+           head_mask, pick, half_mask, output_weight, text_states):
     dma = pltpu.SemaphoreType.DMA
     vmem = pl.BlockSpec(memory_space=pltpu.VMEM)
     smem = pl.BlockSpec(memory_space=pltpu.SMEM)
     low = jnp.bfloat16
     rows = cotangent.shape[0]
-    text = queries.shape[0]
+    text = queries.shape[1]
     return pl.pallas_call(
         finish_kernel,
-        out_shape=(jax.ShapeDtypeStruct((4, 40, 640), jnp.float32),
-                   jax.ShapeDtypeStruct((text, 256), jnp.float32)),
-        in_specs=[smem, smem] + [vmem] * 12 + [pl.BlockSpec(memory_space=pl.ANY)],
-        out_specs=[vmem] * 2,
+        out_shape=(jax.ShapeDtypeStruct((40, 1920), jnp.float32),
+                   jax.ShapeDtypeStruct((20, 1280), jnp.float32),
+                   jax.ShapeDtypeStruct((text, 256), low)),
+        in_specs=[smem] * 3 + [vmem] * 12 + [pl.BlockSpec(memory_space=pl.ANY)] * 2,
+        out_specs=[vmem] * 3,
         scratch_shapes=[
-            pltpu.VMEM((2, 8, 2, rows + 16, 256), low), pltpu.VMEM((2 * text, 32 * 128), jnp.float32),
+            pltpu.VMEM((2, 4, rows + 16, 256), low), pltpu.VMEM((8 * text, 8 * 128), jnp.float32),
             pltpu.VMEM((2, 2, 4, 8, 40, 640), low), pltpu.VMEM((2, 8, 2, text, 256), low),
             pltpu.VMEM((EH * rows, 640), low), pltpu.VMEM((EH * rows, 640), low),
-            pltpu.VMEM(output_weight.shape, low), dma(()),
+            pltpu.VMEM(output_weight.shape, low), pltpu.VMEM((4, 40, 640), jnp.float32),
+            pltpu.VMEM((text, 256), jnp.float32), pltpu.VMEM((text, 256), low),
+            pltpu.VMEM((3, 2 * text, HD), low), pltpu.VMEM((3, 2 * text, HD), low),
+            pltpu.VMEM((3, 8, 2 * text), jnp.float32), pltpu.VMEM((3, 8, 2 * text), jnp.float32),
+            dma((3,)), dma((3,)), dma((3,)), dma((3,)), dma((2,)),
         ] + exchange_scratch() + reduce_scratch() + attended_scratch(),
         compiler_params=pltpu.CompilerParams(
             collective_id=1, has_side_effects=True, vmem_limit_bytes=60 * 2**20),
         name="finish",
-    )(count, length, kv, queries, normed, qkv, probs, spread, out_weight, cotangent, mask_ids,
-      head_mask, pick, half_mask, output_weight)
+    )(count, length, gate, kv, queries, normed, qkv, probs, spread, out_weight, cotangent, mask_ids,
+      head_mask, pick, half_mask, output_weight, text_states)
 
 
 def per_device(
@@ -766,22 +844,13 @@
     kv_weight,
     output_weight,
 ):
-    fsdp_index = lax.axis_index("fsdp")
     head_mask, pick, half_mask = tables()
-    out_halves = jnp.transpose(out_weight.reshape(-1, 2, 640), (1, 0, 2)).reshape(-1, 640)
-    joint = jnp.concatenate([qkv_weight, out_halves], axis=1)
     kv, queries, normed, qkv, probs, spread, out_rows = encode(
-        tile_counts, patches, ln_gain[None], joint, kv_weight, text_states, query_weight,
+        tile_counts, patches, ln_gain, qkv_weight, out_weight, kv_weight, text_states, query_weight,
         head_mask, pick, half_mask)
-    sums, attended = finish(
-        tile_counts, text_lengths, kv, queries, normed, qkv, probs, spread, out_rows, cotangent,
-        mask_ids[:, None], head_mask, pick, half_mask, output_weight)
-    sum_qkv = jnp.transpose(sums[:3], (1, 0, 2)).reshape(40, 1920)
-    sum_out = jnp.transpose(sums[3].reshape(2, 20, 640), (1, 0, 2)).reshape(20, 1280)
-    col_width = attended.shape[1]
-    text_cols = lax.dynamic_slice_in_dim(text_states, fsdp_index * col_width, col_width, 1)
-    result = text_cols.astype(jnp.float32) + jnp.tanh(gate_value[0]) * attended
-    return (sum_qkv, sum_out, result.astype(jnp.bfloat16))
+    return finish(
+        tile_counts, text_lengths, gate_value, kv, queries, normed, qkv, probs, spread, out_rows,
+        cotangent, mask_ids, head_mask, pick, half_mask, output_weight, text_states)
 
 
 def solution(mesh):

time: 172 us -> 138 us (0.80)
  Pallas kernels: 160 us -> 130 us
  other arithmetic: 3.17 us -> 0 us
    pallas_call x1, Pallas kernels: 89.4 us -> 73.2 us  [finish(): pl.pallas_call(finish_kernel, out_shape=(jax.ShapeDtypeStruct((40, 1920),...]
    pallas_call x1, Pallas kernels: 70.2 us -> 57.3 us  [encode(): pl.pallas_call(encode_kernel, out_shape=(jax.ShapeDtypeStruct((KVH, rows...]
    unnamed x5 -> x3, local copies, waits for them, and re-layouts: 1.69 us -> 4.73 us
    broadcast_in_dim x2 -> x0, local copies, waits for them, and re-layouts: 2.03 us -> none  [the longest x1 1.29 us: per_device(): ln_gain[None]]
where the time goes in v4:
time: 138 us
  Pallas kernels  130 us (94%)
  local copies, waits for them, and re-layouts  4.73 us (3%)
  between operations  2.59 us (2%)
    pallas_call x1, Pallas kernels, finish(): pl.pallas_call(finish_kernel, out_shape=(jax.ShapeDtypeStruct((40, 1920),...  73.2 us
    pallas_call x1, Pallas kernels, encode(): pl.pallas_call(encode_kernel, out_shape=(jax.ShapeDtypeStruct((KVH, rows...  57.3 us
    unnamed x3, local copies, waits for them, and re-layouts  4.73 us

profile of v4, /device:TPU:1, one launch (start us, length us, event | category | flops | bytes accessed | tf_op | source)
XLA Modules:
  0.0 137.8 jit_solution(15874136556543515848)
XLA Ops:
  2.6 57.3 %encode.1 = (bf16[8,144,256]{2,1,0:T(8,128)(2,1)}, bf16[4,128,256]{2,1,0:T(8,128)(2,1)}, bf16[128,1280]{1,0:T(8,128)(2,1)}, bf16[3,128,640]{2,1,0:T(8,128)(2,1)}...) custom-call(s32[1]{0:T(128)S(6)} %copy.22.count_ref, bf16[128,1280]{1,0:T(8,128)(2,1)} %patches.1, ...), custom_call_target="tpu_custom_call" | custom-call | tf_op jit(solution)/shard_map/encode/pallas_call | solution.py:319
  59.9 73.2 %finish.1 = (f32[40,1920]{1,0:T(8,128)}, f32[20,1280]{1,0:T(8,128)}, bf16[128,256]{1,0:T(8,128)(2,1)}) custom-call(s32[1]{0:T(128)S(6)} %copy.22.count_ref, s32[1]{0:T(128)S(6)} %copy.23.length_ref, f32[1]{0:T(128)S(6)} %copy.24.gate_ref, bf16[8,144,256]{2,1,0:T(8,128)(2,1)} %get-tuple-element.10.kv, bf16[4,128,256]{2,1,0:T(8,128)(2,1)} %get-tuple-element.11.queries, ...), custom_call_target="tpu_custom_call" | custom-call | tf_op jit(solution)/shard_map/finish/pallas_call | solution.py:808
  133.0 1.7 %copy.25 = f32[40,1920]{1,0:T(8,128)} copy(f32[40,1920]{1,0:T(8,128)} %get-tuple-element.20) | data formatting | bytes 614400
  134.7 1.6 %copy.26 = f32[20,1280]{1,0:T(8,128)} copy(f32[20,1280]{1,0:T(8,128)} %get-tuple-element.21) | data formatting | bytes 204800
  136.3 1.5 %copy.27 = bf16[128,256]{1,0:T(8,128)(2,1)} copy(bf16[128,256]{1,0:T(8,128)(2,1)} %get-tuple-element.22) | data formatting | bytes 131072

commit v5 on v4

v5 whole, which is shorter than its diff:
```python
import jax
import jax.numpy as jnp
import numpy as np
from jax import lax
from jax.sharding import PartitionSpec as P
from jax.experimental import pallas as pl
from jax.experimental.pallas import tpu as pltpu

EH = 8
EHD = 80
PATCH = 32
HD = 128
KVH = 8
LAG = 4
NEAR_LAG = 2
FAR_LAG = 2
KV_AT = 1
REDUCE_AT = 8

EPS = 1e-05
NEG = -1e30

MESH = pl.DeviceIdType.MESH


def place():
    dp = lax.axis_index("dp")
    f = lax.axis_index("fsdp")
    x = lax.rem(dp, 4)
    y = (f // 16) * 2 + dp // 4
    z = lax.rem(f // 2, 8)
    return x, y, z, lax.rem(f, 2)


def device(x, y, z, core):
    return (lax.rem(y, 2) * 4 + x, (y // 2) * 16 + z * 2 + core)


def meet(peers):
    barrier = pltpu.get_barrier_semaphore()
    for peer in peers:
        pl.semaphore_signal(barrier, inc=1, device_id=peer, device_id_type=MESH)
    pl.semaphore_wait(barrier, len(peers))


def remote(src, dst, send_sem, recv_sem, peer):
    return pltpu.make_async_remote_copy(
        src_ref=src, dst_ref=dst, send_sem=send_sem, recv_sem=recv_sem,
        device_id=peer, device_id_type=MESH,
    )


def gather_scratch():
    dma = pltpu.SemaphoreType.DMA
    return [
        dma((2, 2)), dma((2, 2)), dma((2, 8)), dma((2, 8)),
        dma((2, 2, 8)), dma((2, 2, 8)), dma((2, 8)), dma((2, 8)), dma((2, 8)), dma((2, 8)),
    ]


def gather_steps(t, shard, full, pair, init_send, init_recv, z_send, z_recv, near_send, near_recv,
                 far_send, far_recv, core_send, core_recv):
    x, y, z, core = place()
    y_hi = y // 2
    partner = device(x, y, z, 1 - core)
    width = pair.shape[2]
    sign = 1 - 2 * t
    mine = core == y_hi

    def turned(where):
        return lax.rem(where + t, 2)

    def spot_at(where, my_y):
        return my_y + turned(where) * (x - my_y)

    def columns(spot):
        if t == 0:
            return shard.at[spot]
        return shard.at[:, pl.ds(pl.multiple_of(spot * width, 128), width)]

    def unit_z(u):
        d = (u + 1) // 2 if u % 2 else -(u // 2)
        return lax.rem(z - sign * d + 8, 8)

    def along_z(step):
        return device(x, y, lax.rem(z + step + 8, 8), core)

    def along(where, step):
        by_x = turned(where)
        return device(lax.rem(x + by_x * step + 4, 4), lax.rem(y + (1 - by_x) * step + 4, 4), z, core)

    def unit(u, d):
        where = unit_z(u)
        return full.at[lax.rem(spot_at(where, y) + d, 4), core, where]

    def to_partner():
        return remote(columns(spot_at(z, y)), pair.at[core], init_send.at[t, 0],
                      init_recv.at[t, core], partner)

    def to_mirror():
        return remote(columns(spot_at(z, 3 - y)), pair.at[core], init_send.at[t, 1],
                      init_recv.at[t, core], device(x, 3 - y, z, y_hi))

    def own_copy():
        return pltpu.make_async_copy(columns(spot_at(z, y)), pair.at[core], init_send.at[t, 0])

    def from_core(other):
        return remote(pair.at[other], pair.at[other], init_send.at[t, 0], init_recv.at[t, other], partner)

    def z_copy(u, u_next):
        src = unit(u, 0)
        step = sign if u_next % 2 else -sign
        return remote(src, src, z_send.at[t, u_next], z_recv.at[t, u_next], along_z(step))

    def near_copy(side, u):
        src = unit(u, 0)
        return remote(src, src, near_send.at[t, side, u], near_recv.at[t, side, u],
                      along(unit_z(u), 1 - 2 * side))

    def near_arrival(side, u):
        dst = unit(u, 3 - 2 * side)
        return remote(dst, dst, near_send.at[t, side, u], near_recv.at[t, side, u], partner)

    def far_copy(u):
        where = unit_z(u)
        back = lax.rem(where // 2, 2)
        src = unit(u, 3 - 2 * back)
        return remote(src, src, far_send.at[t, u], far_recv.at[t, u], along(where, 1 - 2 * back))

    def far_arrival(u):
        dst = unit(u, 2)
        return remote(dst, dst, far_send.at[t, u], far_recv.at[t, u], partner)

    def pass_on(u):
        src = full.at[:, core, unit_z(u)]
        return remote(src, src, core_send.at[t, u], core_recv.at[t, u], partner)

    def passed(u):
        dst = full.at[:, 1 - core, unit_z(u)]
        return remote(dst, dst, core_send.at[t, u], core_recv.at[t, u], partner)

    to_mirror().start()

    @pl.when(mine)
    def _():
        own_copy().start()

    @pl.when(jnp.logical_not(mine))
    def _():
        to_partner().start()
    yield
    for u in range(8 + NEAR_LAG + FAR_LAG):
        if u == 0:
            @pl.when(mine)
            def _():
                own_copy().wait()
                from_core(1 - core).wait_recv()

            @pl.when(jnp.logical_not(mine))
            def _():
                from_core(0).wait_recv()
                from_core(1).wait_recv()
            both = jnp.concatenate([pair[0].astype(jnp.float32), pair[1].astype(jnp.float32)], axis=0)
            full[spot_at(z, y), core, z] = both.astype(jnp.bfloat16)
            z_copy(0, 1).start()
            z_copy(0, 2).start()
        elif u < 8:
            z_copy(u, u).wait_recv()
            if u + 2 < 8:
                z_copy(u, u + 2).start()
        if u < 8:
            near_copy(0, u).start()
            near_copy(1, u).start()
        if 0 <= u - NEAR_LAG < 8:
            for side in range(2):
                near_arrival(side, u - NEAR_LAG).wait_recv()
            far_copy(u - NEAR_LAG).start()
        if 0 <= u - NEAR_LAG - FAR_LAG:
            far_arrival(u - NEAR_LAG - FAR_LAG).wait_recv()
            pass_on(u - NEAR_LAG - FAR_LAG).start()
        yield
    to_mirror().wait_send()

    @pl.when(jnp.logical_not(mine))
    def _():
        to_partner().wait_send()
    for u in range(8):
        passed(u).wait_recv()
        pass_on(u).wait_send()
        if u:
            z_copy(0, u).wait_send()
        near_copy(0, u).wait_send()
        near_copy(1, u).wait_send()
        far_copy(u).wait_send()
    yield


def dot(a, b, over=((1,), (0,))):
    return lax.dot_general(a, b, (over, ((), ())), preferred_element_type=jnp.float32)


def head_stack(rows, head_mask):
    return jnp.concatenate([rows * head_mask[h:h + 1] for h in range(EH)], axis=0)


def head_pick(stack, head_mask):
    rows = stack.shape[0] // EH
    total = jnp.zeros((rows, stack.shape[1]), jnp.float32)
    for h in range(EH):
        total = total + stack[h * rows:(h + 1) * rows] * head_mask[h:h + 1].astype(jnp.float32)
    return total


def query_copy(queries, send_sem, recv_sem, offset):
    x, y, z, core = place()
    side = lax.rem(z, 2)
    peer = device(x, y, z + (offset // 2) * (1 - 2 * side), lax.rem(core + offset, 2))
    slot = queries.at[2 * side + core]
    return remote(slot, slot, send_sem.at[offset - 1], recv_sem.at[offset - 1], peer)


def reduce_peers():
    x, y, z, core = place()
    peers = [device(x, y, z, 1 - core)]
    for step in range(1, 4):
        for other in range(2):
            peers.append(device(x, lax.rem(y + step, 4), z, other))
            peers.append(device(lax.rem(x + step, 4), y, z, other))
    for step in range(1, 8):
        peers.append(device(x, y, lax.rem(z + step, 8), core))
    return peers


def reduce_steps(grads, out, from_core, chip_sum, from_near, plane_sum, from_z, from_cross, total,
                 core_send, core_recv, near_send, near_recv, z_send, z_recv, cross_send, cross_recv,
                 last_send, last_recv):
    x, y, z, core = place()
    y_hi = y // 2
    partner = device(x, y, z, 1 - core)
    spots = (y, x)
    low = jnp.bfloat16

    def along(axis, step):
        if axis == 0:
            return device(x, lax.rem(y + step, 4), z, core)
        return device(lax.rem(x + step, 4), y, z, core)

    def part(v, d):
        return lax.rem(spots[v] + d, 4)

    def core_copy(v, d):
        return remote(grads.at[1 - core, v, part(v, d)], from_core.at[v, d],
                      core_send.at[v, d], core_recv.at[v, d], partner)

    def near_copy(v, d, h):
        return remote(chip_sum.at[v, d - 1, h], from_near.at[v, d - 1, h],
                      near_send.at[v, d - 1, h], near_recv.at[v, d - 1, h], along(v, d))

    def z_copy(v, d):
        to_z = lax.rem(z + d, 8)
        return remote(plane_sum.at[v, lax.rem(to_z, 2), to_z // 2], from_z.at[v, d],
                      z_send.at[v, d], z_recv.at[v, d], device(x, y, to_z, core))

    def cross_copy(v, d):
        slot = spots[1 - v]
        return remote(from_cross.at[v, slot], from_cross.at[v, slot],
                      cross_send.at[v, d - 1], cross_recv.at[v, d - 1], along(1 - v, d))

    def cross_arrival(v, d):
        slot = lax.rem(spots[1 - v] + 4 - d, 4)
        return remote(from_cross.at[v, slot], from_cross.at[v, slot],
                      cross_send.at[v, d - 1], cross_recv.at[v, d - 1], partner)

    def last_copy(v, i):
        peer = device(x, 2 * core + i, z, 0) if v == 0 else device(i, y, z, 1)
        slot = spots[v]
        return remote(total.at[v], out.at[slot], last_send.at[v, i], last_recv.at[slot], peer)

    def last_self(v, i):
        if v == 0:
            return jnp.logical_and(2 * core + i == y, core == 0)
        return jnp.logical_and(i == x, core == 1)

    for d in (2, 1, 3, 0):
        for v in range(2):
            core_copy(v, d).start()
    yield
    for h in range(2):
        for d in (2, 1, 3):
            for v in range(2):
                if h == 0:
                    core_copy(v, d).wait_recv()

                def add(k, carry, v=v, d=d, h=h):
                    chip_sum[v, d - 1, h, k] = (
                        grads[core, v, part(v, d), 2 * k + h].astype(jnp.float32)
                        + from_core[v, d, 2 * k + h].astype(jnp.float32)
                    ).astype(low)
                    return carry
                lax.fori_loop(0, 4, add, 0)
                near_copy(v, d, h).start()
        yield
    for h in range(2):
        for v in range(2):
            if h == 0:
                core_copy(v, 0).wait_recv()
            for d in range(1, 4):
                near_copy(v, d, h).wait_recv()

            def add(k, carry, v=v, h=h):
                sums = (grads[core, v, spots[v], 2 * k + h].astype(jnp.float32)
                        + from_core[v, 0, 2 * k + h].astype(jnp.float32))
                for d in range(3):
                    sums = sums + from_near[v, d, h, k].astype(jnp.float32)
                plane_sum[v, h, k] = sums.astype(low)
                return carry
            lax.fori_loop(0, 4, add, 0)
            for m in (2, 1, 3, 0):
                step = 2 * m + lax.rem(h + z, 2)

                @pl.when(step != 0)
                def _(v=v, step=step):
                    z_copy(v, step).start()
        yield
    for v in range(2):
        for d in range(1, 8):
            z_copy(v, d).wait_recv()
        sums = plane_sum[v, lax.rem(z, 2), z // 2].astype(jnp.float32)
        for d in range(1, 8):
            sums = sums + from_z[v, d].astype(jnp.float32)
        from_cross[v, spots[1 - v]] = sums.astype(low)
        for d in (2, 1, 3):
            cross_copy(v, d).start()
    yield
    for v in range(2):
        for d in range(1, 4):
            cross_arrival(v, d).wait_recv()
        terms = [from_cross[v, k].astype(jnp.float32) for k in range(4)]
        total[v] = ((terms[0] + terms[1]) + (terms[2] + terms[3])).astype(low)
        for i in range(2 if v == 0 else 4):
            active = True if v == 0 else y_hi == core

            @pl.when(jnp.logical_and(active, jnp.logical_not(last_self(v, i))))
            def _(v=v, i=i):
                last_copy(v, i).start()

            @pl.when(jnp.logical_and(active, last_self(v, i)))
            def _(v=v):
                out[spots[v]] = total[v]
    yield
    for j in range(4):
        skip = jnp.where(core == 0, jnp.logical_and(j == y, y_hi == 0),
                         jnp.logical_and(j == x, y_hi == 1))

        @pl.when(jnp.logical_not(skip))
        def _(j=j):
            remote(out.at[j], out.at[j], last_send.at[0, 0], last_recv.at[j], partner).wait_recv()
    for v in range(2):
        for d in range(4):
            core_copy(v, d).wait_send()
        for d in range(1, 4):
            near_copy(v, d, 0).wait_send()
            near_copy(v, d, 1).wait_send()
            cross_copy(v, d).wait_send()
        for d in range(1, 8):
            z_copy(v, d).wait_send()
        for i in range(2 if v == 0 else 4):
            active = True if v == 0 else y_hi == core

            @pl.when(jnp.logical_and(active, jnp.logical_not(last_self(v, i))))
            def _(v=v, i=i):
                last_copy(v, i).wait_send()


def reduce_scratch():
    dma = pltpu.SemaphoreType.DMA
    block = (40, 640)
    low = jnp.bfloat16
    return [
        pltpu.VMEM((2, 4, 8) + block, low),
        pltpu.VMEM((2, 3, 2, 4) + block, low),
        pltpu.VMEM((2, 3, 2, 4) + block, low),
        pltpu.VMEM((2, 2, 4) + block, low),
        pltpu.VMEM((2, 8) + block, low),
        pltpu.VMEM((2, 4) + block, low),
        pltpu.VMEM((2,) + block, low),
        dma((2, 4)), dma((2, 4)), dma((2, 3, 2)), dma((2, 3, 2)), dma((2, 8)), dma((2, 8)),
        dma((2, 3)), dma((2, 3)), dma((2, 4)), dma((4,)),
    ]


def attended_steps(partial, out, from_core, chip_sum, from_y, group_sum, from_z,
                   core_send, core_recv, y_send, y_recv, z_send, z_recv):
    x, y, z, core = place()
    y_hi = y // 2
    partner = device(x, y, z, 1 - core)
    across = device(x, lax.rem(y + 2, 4), z, core)
    order = (4, 3, 5, 2, 6, 1, 7, 0)

    def spot(d):
        return lax.rem(z + d, 8)

    def core_copy(half, d):
        row = y_hi if half else 1 - y_hi
        return remote(partial.at[row * 16 + spot(d) * 2 + 1 - core], from_core.at[half, d],
                      core_send.at[half, d], core_recv.at[half, d], partner)

    def y_copy(d):
        return remote(chip_sum.at[d], from_y.at[d], y_send.at[d], y_recv.at[d], across)

    def z_copy(d):
        return remote(group_sum.at[d], from_z.at[d], z_send.at[d], z_recv.at[d],
                      device(x, y, spot(d), core))

    for half in range(2):
        for d in order:
            core_copy(half, d).start()
    yield
    for d in order:
        core_copy(0, d).wait_recv()
        chip_sum[d] = (partial[(1 - y_hi) * 16 + spot(d) * 2 + core].astype(jnp.float32)
                       + from_core[0, d].astype(jnp.float32)).astype(jnp.bfloat16)
        y_copy(d).start()
    yield
    for d in order:
        core_copy(1, d).wait_recv()
        y_copy(d).wait_recv()
        sums = (partial[y_hi * 16 + spot(d) * 2 + core].astype(jnp.float32)
                + from_core[1, d].astype(jnp.float32) + from_y[d].astype(jnp.float32))
        if d:
            group_sum[d] = sums.astype(jnp.bfloat16)
            z_copy(d).start()
        else:
            out[...] = sums
    yield
    sums = out[...]
    for d in range(1, 8):
        z_copy(d).wait_recv()
        sums = sums + from_z[d].astype(jnp.float32)
    out[...] = sums
    for d in range(8):
        core_copy(0, d).wait_send()
        core_copy(1, d).wait_send()
        y_copy(d).wait_send()
        if d:
            z_copy(d).wait_send()


def attended_scratch():
    dma = pltpu.SemaphoreType.DMA
    block = (128, 256)
    return [
        pltpu.VMEM((2, 8) + block, jnp.bfloat16),
        pltpu.VMEM((8,) + block, jnp.bfloat16),
        pltpu.VMEM((8,) + block, jnp.bfloat16),
        pltpu.VMEM((8,) + block, jnp.bfloat16),
        pltpu.VMEM((8,) + block, jnp.bfloat16),
        dma((2, 8)), dma((2, 8)), dma((8,)), dma((8,)), dma((8,)), dma((8,)),
    ]


NEAREST = ((0, 0), (1, 0), (0, 1), (1, 1), (2, 0), (2, 1), (3, 0), (3, 1))


def image_at(step, turn):
    x, y, z, core = place()
    from_z = lax.rem(z + (2 * lax.rem(z, 2) - 1) * step + 8, 8)
    return lax.rem(y // 2 + turn, 2) * 16 + from_z * 2 + core


def exchange_steps(kv, arrived, local_sem, far_send, far_recv):
    x, y, z, core = place()

    def far_copy(step, turn):
        to_y = lax.rem(y + 2 * turn, 4)
        to_z = lax.rem(z + step * (1 - 2 * lax.rem(z + step, 2)) + 8, 8)
        head = (to_y // 2) * 4 + to_z // 2
        return remote(kv.at[head], arrived.at[turn, step], far_send.at[turn, step],
                      far_recv.at[turn, step], device(x, to_y, to_z, core))

    own = pltpu.make_async_copy(kv.at[(y // 2) * 4 + z // 2], arrived.at[0, 0], local_sem)
    own.start()
    for step, turn in reversed(NEAREST):
        if step or turn:
            far_copy(step, turn).start()
    yield
    for step, turn in NEAREST:
        if step or turn:
            far_copy(step, turn).wait_recv()
        else:
            own.wait()
        yield
    for step, turn in NEAREST:
        if step or turn:
            far_copy(step, turn).wait_send()


def exchange_scratch():
    dma = pltpu.SemaphoreType.DMA
    return [dma(()), dma((2, 4)), dma((2, 4))]


def tables():
    lane = np.arange(640)
    row = np.arange(1280)
    head_mask = (lane[None] // 80 == np.arange(8)[:, None])
    pick = (row[:, None] // 40 * 20 + row[:, None] % 20) == lane[None]
    half_mask = (row[None] % 40 // 20) == np.arange(2)[:, None]
    return tuple(jnp.asarray(a, jnp.bfloat16) for a in (head_mask, pick, half_mask))


def load_blocks(text, query_weight, texts, weights, sem):
    def start(k, carry):
        columns = pl.ds(pl.multiple_of(k * 256, 256), 256)
        pltpu.make_async_copy(text.at[:, columns], texts.at[k], sem.at[0]).start()
        return carry
    pltpu.make_async_copy(query_weight, weights, sem.at[1]).start()
    lax.fori_loop(0, 32, start, 0)


def step_kernel(count_ref, length_ref, gate_ref, patches, cotangent, gain, qkv_shard, out_shard, kv_shard,
                mask_ids, head_mask, pick, half_mask, text, query_weight, output_weight,
                sums, result_out,
                joint, joint_full, kv_full, joint_pair, kv_pair, texts, weights, kv, queries, normed, qkv,
                probs_ref, spread, arrived, scores, grads, head_rows, grad_rows, attended, text_in,
                part_out, part_in, stat_out, stat_in, part_send, part_recv, stat_send, stat_recv,
                query_send, query_recv, load_sem, *rest):
    a = len(gather_scratch())
    b = a + len(exchange_scratch())
    c = b + len(reduce_scratch())
    low = jnp.bfloat16
    x, y, z, core = place()
    side = lax.rem(z, 2)
    for part in range(3):
        joint[part] = qkv_shard[:, part * 640:(part + 1) * 640]
    shard = out_shard[...].astype(jnp.float32)
    joint[3] = jnp.concatenate([shard[:, :640], shard[:, 640:]], axis=0).astype(low)
    meet(step_peers())
    first = gather_steps(0, joint, joint_full, joint_pair, *rest[:a])
    second = gather_steps(1, kv_shard, kv_full, kv_pair, *rest[:a])
    exchange = exchange_steps(kv, arrived, *rest[a:b])
    reduce = reduce_steps(grads, sums, *rest[b:c])
    partial = texts
    attend = attended_steps(partial, attended, *rest[c:])
    next(first)
    next(second)
    load_blocks(text, query_weight, texts, weights, load_sem)
    columns = pl.ds(pl.multiple_of(lax.axis_index("fsdp") * 256, 256), 256)
    load_text = pltpu.make_async_copy(text.at[:, columns], text_in, load_sem.at[2])
    load_text.start()

    next(first)
    inputs = patches[...].astype(jnp.float32)
    rows = inputs.shape[0]
    centred = inputs - jnp.mean(inputs, axis=-1, keepdims=True)
    variance = jnp.mean(centred * centred, axis=-1, keepdims=True)
    normed[...] = (centred * lax.rsqrt(variance + EPS) * gain[...].reshape(1, -1)).astype(low)
    next(first)
    pltpu.make_async_copy(texts, texts, load_sem.at[0]).wait()
    pltpu.make_async_copy(query_weight, weights, load_sem.at[1]).wait()
    total = jnp.zeros(queries.shape[1:], jnp.float32)
    steps = 6 + NEAR_LAG + FAR_LAG
    for step in range(steps):
        if step < 8:
            for k in range(4 * step, 4 * step + 4):
                total = total + dot(texts[k], weights[k])
        if step == 8:
            queries[2 * side + core] = total.astype(low)
            for offset in range(1, 4):
                query_copy(queries, query_send, query_recv, offset).start()

            def start(k, carry):
                block = pl.ds(pl.multiple_of(k * 256, 256), 256)
                pltpu.make_async_copy(output_weight.at[:, block], weights.at[k], load_sem.at[1]).start()
                return carry
            lax.fori_loop(0, 32, start, 0)
        next(first)
        if step >= LAG:
            next(second, None)
    next(first, None)

    masks = head_mask[...]
    next(second, None)
    query = dot(normed[...], joint_full[0].reshape(1280, 640)).astype(low)
    qkv[0] = query
    next(second, None)
    key = dot(normed[...], joint_full[1].reshape(1280, 640)).astype(low)
    qkv[1] = key
    next(second, None)
    value = dot(normed[...], joint_full[2].reshape(1280, 640)).astype(low)
    qkv[2] = value
    next(second, None)
    live_key = lax.broadcasted_iota(jnp.int32, (1, rows), 1) < count_ref[0] * PATCH
    live_row = lax.broadcasted_iota(jnp.int32, (rows, 1), 0) < count_ref[0] * PATCH
    head_rows[...] = head_stack(query, masks)
    inner_scores = dot(head_rows[...], key, ((1,), (1,))) * EHD ** (-0.5)
    inner_scores = jnp.where(live_key, inner_scores, NEG)
    shares = jnp.exp(inner_scores - jnp.max(inner_scores, axis=-1, keepdims=True))
    probs_ref[...] = shares / jnp.sum(shares, axis=-1, keepdims=True)
    next(second, None)
    context = head_pick(dot(probs_ref[...].astype(low), qkv[2]), masks).astype(low)
    both = dot(context, pick[...], ((1,), (1,))).astype(low)
    spread[...] = jnp.concatenate([both * half_mask[0:1], both * half_mask[1:2]], axis=0)
    next(second, None)
    branch = dot(spread[...], joint_full[3].reshape(1280, 640))
    branch = jnp.concatenate([branch[:rows], branch[rows:]], axis=1)
    vision = jnp.where(live_row, patches[...].astype(jnp.float32) + branch, 0.0).astype(low)
    normed_t = normed[...].T
    next(second, None)

    upstream = jnp.where(live_row, cotangent[...].astype(jnp.float32), 0.0).astype(low)
    sides = jnp.concatenate([upstream[:, :640], upstream[:, 640:]], axis=0)
    backs = dot(sides, joint_full[3].reshape(1280, 640), ((1,), (1,)))
    backs = (backs[:rows] * half_mask[0:1].astype(jnp.float32)
             + backs[rows:] * half_mask[1:2].astype(jnp.float32))
    high = backs.astype(low)
    rest_low = (backs - high.astype(jnp.float32)).astype(low)
    picked = dot(jnp.concatenate([high, rest_low], axis=0), pick[...])
    grad_context = (picked[:rows] + picked[rows:]).astype(low)
    grad_rows[...] = head_stack(grad_context, masks)
    next(second, None)

    def project_kv():
        for part in range(4):
            piece = dot(vision, kv_full[part].reshape(1280, 512)).astype(low)
            for half in range(2):
                kv[2 * part + half, pl.ds(0, rows), :] = piece[:, half * 256:(half + 1) * 256]
        number = jnp.full((KVH, 16, 256), count_ref[0].astype(jnp.float32)).astype(low)
        kv[:, pl.ds(rows, 16), :] = number
        next(exchange)

    if KV_AT == 0:
        for _ in second:
            pass
        project_kv()
    probs = probs_ref[...]
    grad_probs = dot(grad_rows[...], qkv[2], ((1,), (1,)))
    inner = jnp.sum(probs * grad_probs, axis=-1, keepdims=True)
    grad_scores = (probs * (grad_probs - inner) * EHD ** (-0.5)).astype(low)
    next(second, None)
    grad_values = dot(probs.astype(low).T, grad_rows[...]).astype(low)
    grad_keys = dot(grad_scores.T, head_rows[...]).astype(low)
    grad_queries = head_pick(dot(grad_scores, qkv[1]), masks).astype(low)
    if KV_AT == 1:
        for _ in second:
            pass
        project_kv()

    def store(j, left, right):
        for upper in range(2):
            block = dot(left[640 * upper:640 * (upper + 1)], right)
            for k in range(8):
                for other in range(2):
                    at = 80 * k + 40 * other
                    grads[upper, other, j, k] = block[at:at + 40].astype(low)

    for j, right in enumerate((grad_queries, grad_keys, grad_values)):
        store(j, normed_t, right)
        next(second, None)
    store(3, spread[...].T, sides)
    next(reduce)
    next(second, None)
    next(reduce)
    next(second, None)
    next(reduce)
    if KV_AT == 2:
        for _ in second:
            pass
        project_kv()

    for offset in range(1, 4):
        query_copy(queries, query_send, query_recv, offset).wait()
    text_rows = queries.shape[1]
    stacked = jnp.concatenate(
        [queries[g, :, half * HD:(half + 1) * HD] for g in range(4) for half in range(2)], axis=0)
    square = (text_rows, text_rows)
    diagonal = (lax.broadcasted_iota(jnp.int32, square, 0) == lax.broadcasted_iota(jnp.int32, square, 1))
    images = jnp.sum(jnp.where(diagonal, mask_ids[...].astype(jnp.float32).reshape(1, text_rows), 0.0),
                     axis=1, keepdims=True)
    images = jnp.concatenate([images] * 8, axis=0)
    tile_of = lax.broadcasted_iota(jnp.int32, (1, rows), 1).astype(jnp.float32)
    top = jnp.full((8 * text_rows, 1), NEG, jnp.float32)
    for i, (step, turn) in enumerate(NEAREST):
        if i == REDUCE_AT:
            next(reduce)
        next(exchange)
        counts = arrived[turn, step, pl.ds(rows, 16), pl.ds(0, 128)][0:1].astype(jnp.float32)
        number = image_at(step, turn).astype(jnp.float32)
        allowed = jnp.logical_and(tile_of < counts * float(PATCH), number < images)
        piece = dot(stacked, arrived[turn, step, pl.ds(0, rows), pl.ds(0, HD)], ((1,), (1,)))
        piece = jnp.where(allowed, piece * HD ** (-0.5), NEG)
        scores[:, i * 128:(i + 1) * 128] = piece
        top = jnp.maximum(top, jnp.max(piece, axis=-1, keepdims=True))
    total = jnp.zeros((8 * text_rows, 1), jnp.float32)
    context = jnp.zeros((8 * text_rows, HD), jnp.float32)
    for i, (step, turn) in enumerate(NEAREST):
        piece = jnp.exp(scores[:, i * 128:(i + 1) * 128] - top)
        total = total + jnp.sum(piece, axis=-1, keepdims=True)
        context = context + dot(piece.astype(low), arrived[turn, step, pl.ds(0, rows), pl.ds(HD, HD)])
    context = context / total
    total = jnp.where(top > 0.5 * NEG, total, 0.0)
    for _ in exchange:
        pass
    scores[:, 0:128] = context
    lane = lax.broadcasted_iota(jnp.int32, (1, 128), 1)
    scores[:, 128:256] = jnp.where(lane < 4, top, total)

    def own_rows(group):
        return pl.ds(pl.multiple_of(group * 2 * text_rows, 256), 2 * text_rows)

    def merge_copy(offset, out, into, send_sem, recv_sem):
        peer = device(x, y, z + (offset // 2) * (1 - 2 * side), lax.rem(core + offset, 2))
        return remote(out.at[offset - 1], into.at[offset - 1], send_sem.at[offset - 1],
                      recv_sem.at[offset - 1], peer)

    def context_copy(offset):
        return merge_copy(offset, part_out, part_in, part_send, part_recv)

    def stat_copy(offset):
        return merge_copy(offset, stat_out, stat_in, stat_send, stat_recv)

    for offset in (2, 3, 1):
        group = 2 * lax.rem(side + offset // 2, 2) + lax.rem(core + offset, 2)
        part_out[offset - 1] = scores[own_rows(group), 0:128].astype(low)
        context_copy(offset).start()
        stat_out[offset - 1] = scores[own_rows(group), 128:256].T[0:8]
        stat_copy(offset).start()
    if REDUCE_AT == 8:
        next(reduce)
    group = 2 * side + core
    parts = [scores[own_rows(group), 0:128]]
    tops = [scores[own_rows(group), 128:129]]
    totals = [scores[own_rows(group), 132:133]]
    for offset in range(1, 4):
        context_copy(offset).wait_recv()
        stat_copy(offset).wait_recv()
        stats = jnp.concatenate([stat_in[offset - 1]] * 16, axis=0).T
        parts.append(part_in[offset - 1].astype(jnp.float32))
        tops.append(stats[:, 0:1])
        totals.append(stats[:, 4:5])
    top = jnp.maximum(jnp.maximum(tops[0], tops[1]), jnp.maximum(tops[2], tops[3]))
    seen = jnp.zeros((2 * text_rows, 1), jnp.float32)
    context = jnp.zeros((2 * text_rows, HD), jnp.float32)
    for k in range(4):
        share = totals[k] * jnp.exp(tops[k] - top)
        seen = seen + share
        context = context + share * parts[k]
    context = (context / jnp.where(seen > 0.0, seen, 1.0)).astype(low)
    context = jnp.concatenate([context[:text_rows], context[text_rows:]], axis=1)
    pltpu.make_async_copy(weights, weights, load_sem.at[1]).wait()

    def project(block, carry):
        partial[block] = dot(context, weights[block]).astype(low)
        return carry
    lax.fori_loop(0, 32, project, 0)
    next(attend)
    if REDUCE_AT == 9:
        next(reduce)
    next(attend)
    next(reduce)
    next(attend)
    next(reduce)
    for _ in attend:
        pass
    for _ in reduce:
        pass
    for offset in range(1, 4):
        context_copy(offset).wait_send()
        stat_copy(offset).wait_send()
    rows_live = jnp.logical_and(
        seen[:text_rows] > 0.0,
        lax.broadcasted_iota(jnp.int32, (text_rows, 1), 0) < length_ref[0])
    gate = jnp.tanh(jnp.full((1, 256), gate_ref[0], jnp.float32))
    load_text.wait()
    result_out[...] = (text_in[...].astype(jnp.float32)
                       + gate * jnp.where(rows_live, attended[...], 0.0)).astype(low)


def step_peers():
    x, y, z, core = place()
    peers = reduce_peers()
    for step in range(1, 8):
        peers.append(device(x, lax.rem(y + 2, 4), lax.rem(z + step, 8), core))
    peers.append(device(x, y, z + 1 - 2 * lax.rem(z, 2), 1 - core))
    return peers


def whole_step(*operands):
    dma = pltpu.SemaphoreType.DMA
    vmem = pl.BlockSpec(memory_space=pltpu.VMEM)
    smem = pl.BlockSpec(memory_space=pltpu.SMEM)
    low = jnp.bfloat16
    rows = operands[3].shape[0]
    text = operands[13].shape[0]
    return pl.pallas_call(
        step_kernel,
        out_shape=(jax.ShapeDtypeStruct((4, 40, 640), low),
                   jax.ShapeDtypeStruct((text, 256), low)),
        in_specs=[smem] * 3 + [vmem] * 10 + [pl.BlockSpec(memory_space=pl.ANY)] * 3,
        out_specs=[vmem] * 2,
        scratch_shapes=[
            pltpu.VMEM((4, 40, 640), low), pltpu.VMEM((4, 2, 8, 80, 640), low),
            pltpu.VMEM((4, 2, 8, 80, 512), low), pltpu.VMEM((2, 40, 640), low),
            pltpu.VMEM((2, 40, 512), low), pltpu.VMEM((32, text, 256), low),
            pltpu.VMEM((32, 256, 256), low), pltpu.VMEM((KVH, rows + 16, 256), low),
            pltpu.VMEM((4, text, 256), low), pltpu.VMEM((rows, 1280), low),
            pltpu.VMEM((3, rows, 640), low), pltpu.VMEM((EH * rows, rows), jnp.float32),
            pltpu.VMEM((2 * rows, 1280), low), pltpu.VMEM((2, 4, rows + 16, 256), low),
            pltpu.VMEM((8 * text, 8 * 128), jnp.float32), pltpu.VMEM((2, 2, 4, 8, 40, 640), low),
            pltpu.VMEM((EH * rows, 640), low), pltpu.VMEM((EH * rows, 640), low),
            pltpu.VMEM((text, 256), jnp.float32), pltpu.VMEM((text, 256), low),
            pltpu.VMEM((3, 2 * text, HD), low), pltpu.VMEM((3, 2 * text, HD), low),
            pltpu.VMEM((3, 8, 2 * text), jnp.float32), pltpu.VMEM((3, 8, 2 * text), jnp.float32),
            dma((3,)), dma((3,)), dma((3,)), dma((3,)), dma((3,)), dma((3,)), dma((3,)),
        ] + gather_scratch() + exchange_scratch() + reduce_scratch() + attended_scratch(),
        compiler_params=pltpu.CompilerParams(
            collective_id=0, has_side_effects=True, vmem_limit_bytes=63 * 2**20),
        name="whole_step",
    )(*operands)


def result_kernel(sums, result, qkv_out, out_out, result_out):
    for j in range(3):
        qkv_out[:, j * 640:(j + 1) * 640] = sums[j].astype(jnp.float32)
    last = sums[3].astype(jnp.float32)
    out_out[:, 0:640] = last[0:20]
    out_out[:, 640:1280] = last[20:40]
    result_out[...] = result[...]


def write_results(sums, result):
    vmem = pl.BlockSpec(memory_space=pltpu.VMEM)
    return pl.pallas_call(
        result_kernel,
        out_shape=(jax.ShapeDtypeStruct((40, 1920), jnp.float32),
                   jax.ShapeDtypeStruct((20, 1280), jnp.float32),
                   jax.ShapeDtypeStruct(result.shape, result.dtype)),
        in_specs=[vmem] * 2,
        out_specs=[vmem] * 3,
        name="write_results",
    )(sums, result)


def per_device(
    patches,
    cotangent,
    tile_counts,
    ln_gain,
    qkv_weight,
    out_weight,
    text_states,
    mask_ids,
    text_lengths,
    gate_value,
    query_weight,
    kv_weight,
    output_weight,
):
    head_mask, pick, half_mask = tables()
    sums, result = whole_step(
        tile_counts, text_lengths, gate_value, patches, cotangent, ln_gain, qkv_weight, out_weight,
        kv_weight, mask_ids, head_mask, pick, half_mask, text_states,
        query_weight.reshape(32, 256, 256), output_weight)
    return write_results(sums, result)


def solution(mesh):
    placed = (
        P(("dp", "fsdp"), None),
        P(("dp", "fsdp"), None),
        P(("dp", "fsdp")),
        P(),
        P("fsdp", None),
        P("fsdp", None),
        P("dp", None),
        P("dp"),
        P("dp"),
        P(),
        P(None, "fsdp"),
        P("fsdp", None),
        P("fsdp", None),
    )
    return jax.shard_map(
        per_device,
        mesh=mesh,
        in_specs=placed,
        out_specs=(P("fsdp", None), P("fsdp", None), P("dp", "fsdp")),
        check_vma=False,
    )
```

time: 138 us -> 132 us (0.957)
  local copies, waits for them, and re-layouts: 4.73 us -> 0 us
    unnamed x3 -> x0, local copies, waits for them, and re-layouts: 4.73 us -> none
where the time goes in v5:
time: 132 us
  Pallas kernels  130 us (98%)
  between operations  2.58 us (2%)
    pallas_call x1, Pallas kernels, whole_step(): pl.pallas_call(step_kernel, out_shape=(jax.ShapeDtypeStruct((4, 40, 640),...  128 us

profile of v5, /device:TPU:1, one launch (start us, length us, event | category | flops | bytes accessed | tf_op | source)
XLA Modules:
  0.0 132.3 jit_solution(587911355057973256)
XLA Ops:
  2.6 128.0 %whole_step.1 = (bf16[4,40,640]{2,1,0:T(8,128)(2,1)}, bf16[128,256]{1,0:T(8,128)(2,1)}) custom-call(s32[1]{0:T(128)S(6)} %copy.19.count_ref, s32[1]{0:T(128)S(6)} %copy.20.length_ref, f32[1]{0:T(128)S(6)} %copy.21.gate_ref, bf16[128,1280]{1,0:T(8,128)(2,1)} %patches.1, bf16[128,1280]{1,0:T(8,128)(2,1)} %cotangent.1, f32[1280]{0:T(1024)} %gain.1, ...), custom_call_target="tpu_custom_call" | custom-call | tf_op jit(solution)/shard_map/whole_step/pallas_call | solution.py:795
  130.6 1.7 %write_results.1 = (f32[40,1920]{1,0:T(8,128)}, f32[20,1280]{1,0:T(8,128)}, bf16[128,256]{1,0:T(8,128)(2,1)}) custom-call(bf16[4,40,640]{2,1,0:T(8,128)(2,1)} %get-tuple-element.5.sums, bf16[128,256]{1,0:T(8,128)(2,1)} %get-tuple-element.6.result), custom_call_target="tpu_custom_call" | custom-call | tf_op jit(solution)/shard_map/write_results/pallas_call | solution.py:833

commit v6 on v5

--- a/solution.py
+++ b/solution.py
@@ -11,11 +11,12 @@
 PATCH = 32
 HD = 128
 KVH = 8
-LAG = 4
-NEAR_LAG = 2
-FAR_LAG = 2
-KV_AT = 1
+LAG = 0
+NEAR_LAG = 3
+FAR_LAG = 3
+KV_AT = 0
 REDUCE_AT = 8
+GRAD_ORDER = (3, 0, 1, 2)
 
 EPS = 1e-05
 NEG = -1e30
@@ -281,10 +282,10 @@
             return jnp.logical_and(2 * core + i == y, core == 0)
         return jnp.logical_and(i == x, core == 1)
 
-    for d in (2, 1, 3, 0):
+    for j in GRAD_ORDER:
         for v in range(2):
-            core_copy(v, d).start()
-    yield
+            core_copy(v, lax.rem(j - spots[v] + 4, 4)).start()
+        yield
     for h in range(2):
         for d in (2, 1, 3):
             for v in range(2):
@@ -432,6 +433,8 @@
             z_copy(d).start()
         else:
             out[...] = sums
+        if d == 2:
+            yield
     yield
     sums = out[...]
     for d in range(1, 8):
@@ -605,7 +608,6 @@
     branch = dot(spread[...], joint_full[3].reshape(1280, 640))
     branch = jnp.concatenate([branch[:rows], branch[rows:]], axis=1)
     vision = jnp.where(live_row, patches[...].astype(jnp.float32) + branch, 0.0).astype(low)
-    normed_t = normed[...].T
     next(second, None)
 
     upstream = jnp.where(live_row, cotangent[...].astype(jnp.float32), 0.0).astype(low)
@@ -654,14 +656,14 @@
                     at = 80 * k + 40 * other
                     grads[upper, other, j, k] = block[at:at + 40].astype(low)
 
+    store(3, spread[...].T, sides)
+    next(reduce)
+    normed_t = normed[...].T
     for j, right in enumerate((grad_queries, grad_keys, grad_values)):
         store(j, normed_t, right)
+        next(reduce)
         next(second, None)
-    store(3, spread[...].T, sides)
     next(reduce)
-    next(second, None)
-    next(reduce)
-    next(second, None)
     next(reduce)
     if KV_AT == 2:
         for _ in second:
@@ -754,8 +756,8 @@
         return carry
     lax.fori_loop(0, 32, project, 0)
     next(attend)
-    if REDUCE_AT == 9:
-        next(reduce)
+    next(attend)
+    next(reduce)
     next(attend)
     next(reduce)
     next(attend)

time: 132 us -> 125 us (0.947); the launches traced: 132 us -> 123 us
  Pallas kernels: 130 us -> 121 us
    pallas_call x1, Pallas kernels: 128 us -> 119 us  [whole_step(): pl.pallas_call(step_kernel, out_shape=(jax.ShapeDtypeStruct((4, 40, 640),...]
where the time goes in v6:
time: 125 us; the launch traced here: 123 us
  Pallas kernels  121 us (97%)
  between operations  2.58 us (2%)
    pallas_call x1, Pallas kernels, whole_step(): pl.pallas_call(step_kernel, out_shape=(jax.ShapeDtypeStruct((4, 40, 640),...  119 us

profile of v6, /device:TPU:1, one launch (start us, length us, event | category | flops | bytes accessed | tf_op | source)
XLA Modules:
  0.0 123.5 jit_solution(15510635530160353897)
XLA Ops:
  2.6 119.2 %whole_step.1 = (bf16[4,40,640]{2,1,0:T(8,128)(2,1)}, bf16[128,256]{1,0:T(8,128)(2,1)}) custom-call(s32[1]{0:T(128)S(6)} %copy.19.count_ref, s32[1]{0:T(128)S(6)} %copy.20.length_ref, f32[1]{0:T(128)S(6)} %copy.21.gate_ref, bf16[128,1280]{1,0:T(8,128)(2,1)} %patches.1, bf16[128,1280]{1,0:T(8,128)(2,1)} %cotangent.1, f32[1280]{0:T(1024)} %gain.1, ...), custom_call_target="tpu_custom_call" | custom-call | tf_op jit(solution)/shard_map/whole_step/pallas_call | solution.py:797
  121.7 1.7 %write_results.1 = (f32[40,1920]{1,0:T(8,128)}, f32[20,1280]{1,0:T(8,128)}, bf16[128,256]{1,0:T(8,128)(2,1)}) custom-call(bf16[4,40,640]{2,1,0:T(8,128)(2,1)} %get-tuple-element.5.sums, bf16[128,256]{1,0:T(8,128)(2,1)} %get-tuple-element.6.result), custom_call_target="tpu_custom_call" | custom-call | tf_op jit(solution)/shard_map/write_results/pallas_call | solution.py:835

commit v7 on v6

--- a/solution.py
+++ b/solution.py
@@ -751,11 +751,14 @@
     context = jnp.concatenate([context[:text_rows], context[text_rows:]], axis=1)
     pltpu.make_async_copy(weights, weights, load_sem.at[1]).wait()
 
-    def project(block, carry):
-        partial[block] = dot(context, weights[block]).astype(low)
-        return carry
-    lax.fori_loop(0, 32, project, 0)
+    def project(half):
+        for k in range(16):
+            block = 2 * k + half
+            partial[block] = dot(context, weights[block]).astype(low)
+
+    project(1 - core)
     next(attend)
+    project(core)
     next(attend)
     next(reduce)
     next(attend)

time: 125 us -> 123 us (0.984)
  Pallas kernels: 121 us -> 119 us
    pallas_call x1, Pallas kernels: 119 us -> 117 us  [whole_step(): pl.pallas_call(step_kernel, out_shape=(jax.ShapeDtypeStruct((4, 40, 640),...]
where the time goes in v7:
time: 123 us; the launch traced here: 122 us
  Pallas kernels  119 us (97%)
  between operations  2.58 us (2%)
    pallas_call x1, Pallas kernels, whole_step(): pl.pallas_call(step_kernel, out_shape=(jax.ShapeDtypeStruct((4, 40, 640),...  117 us

profile of v7, /device:TPU:1, one launch (start us, length us, event | category | flops | bytes accessed | tf_op | source)
XLA Modules:
  0.0 121.6 jit_solution(8293244607715772083)
XLA Ops:
  2.6 117.3 %whole_step.1 = (bf16[4,40,640]{2,1,0:T(8,128)(2,1)}, bf16[128,256]{1,0:T(8,128)(2,1)}) custom-call(s32[1]{0:T(128)S(6)} %copy.19.count_ref, s32[1]{0:T(128)S(6)} %copy.20.length_ref, f32[1]{0:T(128)S(6)} %copy.21.gate_ref, bf16[128,1280]{1,0:T(8,128)(2,1)} %patches.1, bf16[128,1280]{1,0:T(8,128)(2,1)} %cotangent.1, f32[1280]{0:T(1024)} %gain.1, ...), custom_call_target="tpu_custom_call" | custom-call | tf_op jit(solution)/shard_map/whole_step/pallas_call | solution.py:800
  119.8 1.7 %write_results.1 = (f32[40,1920]{1,0:T(8,128)}, f32[20,1280]{1,0:T(8,128)}, bf16[128,256]{1,0:T(8,128)(2,1)}) custom-call(bf16[4,40,640]{2,1,0:T(8,128)(2,1)} %get-tuple-element.5.sums, bf16[128,256]{1,0:T(8,128)(2,1)} %get-tuple-element.6.result), custom_call_target="tpu_custom_call" | custom-call | tf_op jit(solution)/shard_map/write_results/pallas_call | solution.py:838
